TPU v7x, 512 devices: a whole 4x4x16 slice. The times are simulated.
512 devices in a mesh: section: 8 (over y, core), dp: 64 (over z, x).
Axes of the slice: x: 4, y: 4, z: 16, core: 2. Of those that a mesh axis runs over, the one named last changes fastest.
Arguments:
- source_tokens: bfloat16 [16384, 2048], P('dp'), may hold values from -6 to 6
- send_counts: int32 [64, 64], replicated, may hold values from 0 to 4, as said below
- doc_segments: int32 [256, 32], P('dp'), may hold values from 0 to 7, never falling along the last dimension, each value on 1 to 16 neighbouring positions
- out_cotangent: bfloat16 [8192, 2048], P('dp'), may hold values from -0.01953125 to 0.01953125
- norm_gain: float32 [8, 2048], P('section'), may hold values from 0.25 to 1.75
- query_weight: bfloat16 [8, 2048, 1024], P('section', 'dp'), may hold values from -0.125 to 0.125
- frozen_key_matrix: bfloat16 [8, 2048, 256], P('section', 'dp'), may hold values from -0.125 to 0.125
- frozen_value_matrix: bfloat16 [8, 2048, 256], P('section', 'dp'), may hold values from -0.125 to 0.125
- out_weight: bfloat16 [8, 1024, 2048], P('section', 'dp'), may hold values from -0.1875 to 0.1875
- adapter_down: bfloat16 [8, 2, 2048, 16], P('section'), may hold values from -0.125 to 0.125
- adapter_up_maps: bfloat16 [8, 16, 1280], P('section'), may hold values from -0.1875 to 0.1875
Outputs:
- down_grads: float32 [8, 2, 2048, 16], P('section')
- up_grads: float32 [8, 16, 1280], P('section')
Inputs may be any that keep to these rules, and one draw needn't show every extreme that they name: `send_counts`: entry [s, d] counts tokens from replica s to replica d. Every column holds exactly one entry 4 and at least one entry 0; every column sums to at most 128, and some column sums to exactly that. `doc_segments`: segment ids never fall along a micro-batch; a segment spans at most 16 positions.
All inputs are finite; a program needn't handle non-finite values.
Results may differ from a plain program's by a relative error of at most 0.035.
Values may be sent and summed in bfloat16 or wider, within the bound.
No kernel may reach another device: no remote copies, remote signals or barrier semaphores. Data moves between devices by JAX's collectives and lax.ppermute only.
A program may use at most 64 MiB of HBM per device.

v0:
```python
import jax
import jax.numpy as jnp
from jax import lax
from jax.sharding import PartitionSpec as P

QUERY_HEADS = 16
KEY_VALUE_HEADS = 4
HEAD_SIZE = 64


ROPE_BASE = 500000.0
ADAPTER_SCALE = 2.0
NORM_EPS = 1e-05


def from_behind(block, axis, distance):
    devices = range(lax.axis_size(axis))
    route = [(i - distance, i) for i in devices if i - distance in devices]
    return lax.ppermute(block, axis, route)


def doc_layout(seg_row, valid_row):
    token_row_count = seg_row.shape[0]
    places = jnp.arange(token_row_count, dtype=jnp.int32)
    same_doc = seg_row[:, None] == seg_row[None, :]
    before = places[None, :] < places[:, None]
    position = jnp.sum(jnp.where(same_doc & before, 1.0, 0.0).astype(jnp.float32), axis=1)
    causal = places[None, :] <= places[:, None]
    paired = same_doc & valid_row[:, None] & valid_row[None, :]
    allowed = causal & (paired | (places[None, :] == places[:, None]))
    frequency = ROPE_BASE ** (-2.0 * jnp.arange(HEAD_SIZE // 2, dtype=jnp.float32) / HEAD_SIZE)
    angles = position[:, None] * frequency[None, :]
    return (jnp.cos(angles)[:, None, :], jnp.sin(angles)[:, None, :], allowed)


def normalize(hidden, gain_row):
    energy = jnp.mean(hidden * hidden, axis=-1, keepdims=True)
    return (hidden * lax.rsqrt(energy + NORM_EPS) * gain_row).astype(jnp.bfloat16)


def rotary_apply(tensor, cosine_table, sine_table):
    middle = tensor.shape[-1] // 2
    leading = tensor[..., :middle]
    trailing = tensor[..., middle:]
    return jnp.concatenate(
        [
            leading * cosine_table - trailing * sine_table,
            trailing * cosine_table + leading * sine_table,
        ],
        axis=-1,
    )


def project(normed_hidden, adapter, frozen, cosine_table, sine_table):
    w_query, key_projection_weight, w_value = frozen
    down_pair, up_pair = adapter
    split_at = QUERY_HEADS * HEAD_SIZE
    token_row_count = normed_hidden.shape[0]
    low_query = jnp.dot(normed_hidden, down_pair[0], preferred_element_type=jnp.float32).astype(
        jnp.bfloat16
    )
    low_value = jnp.dot(normed_hidden, down_pair[1], preferred_element_type=jnp.float32).astype(
        jnp.bfloat16
    )
    query_rows = jnp.dot(
        normed_hidden, w_query, preferred_element_type=jnp.float32
    ) + ADAPTER_SCALE * jnp.dot(
        low_query, up_pair[:, :split_at], preferred_element_type=jnp.float32
    )
    query_rows = rotary_apply(
        query_rows.reshape(token_row_count, QUERY_HEADS, HEAD_SIZE), cosine_table, sine_table
    ).astype(jnp.bfloat16)
    key_head_rows = rotary_apply(
        jnp.dot(normed_hidden, key_projection_weight, preferred_element_type=jnp.float32).reshape(
            token_row_count, KEY_VALUE_HEADS, HEAD_SIZE
        ),
        cosine_table,
        sine_table,
    ).astype(jnp.bfloat16)
    value_head_rows = jnp.dot(
        normed_hidden, w_value, preferred_element_type=jnp.float32
    ) + ADAPTER_SCALE * jnp.dot(
        low_value, up_pair[:, split_at:], preferred_element_type=jnp.float32
    )
    value_head_rows = value_head_rows.astype(jnp.bfloat16).reshape(
        token_row_count, KEY_VALUE_HEADS, HEAD_SIZE
    )
    return (query_rows, key_head_rows, value_head_rows)


def attend(query_rows, key_head_rows, value_head_rows, allowed):
    token_row_count = query_rows.shape[0]
    grouped_queries = query_rows.reshape(
        token_row_count, KEY_VALUE_HEADS, QUERY_HEADS // KEY_VALUE_HEADS, HEAD_SIZE
    )
    scores = jnp.einsum(
        "qhgd,khd->hgqk", grouped_queries, key_head_rows, preferred_element_type=jnp.float32
    ) * HEAD_SIZE ** (-0.5)
    weights = jnp.where(allowed[None, None], jnp.exp(scores), 0.0)
    shares = (weights / jnp.sum(weights, axis=-1, keepdims=True)).astype(jnp.bfloat16)
    blended = jnp.einsum(
        "hgqk,khd->qhgd", shares, value_head_rows, preferred_element_type=jnp.float32
    )
    return blended.reshape(token_row_count, QUERY_HEADS * HEAD_SIZE).astype(jnp.bfloat16)


def finish(hidden, blended, w_out):
    return (hidden + jnp.dot(blended, w_out, preferred_element_type=jnp.float32)).astype(
        jnp.bfloat16
    )


def section_apply(tokens, adapter, frozen, gain_row, cosine_table, sine_table, allowed):
    hidden = tokens.astype(jnp.float32)
    normed_hidden = normalize(hidden, gain_row)
    query_rows, key_head_rows, value_head_rows = project(
        normed_hidden, adapter, frozen[:3], cosine_table, sine_table
    )
    return finish(hidden, attend(query_rows, key_head_rows, value_head_rows, allowed), frozen[3])


def back_whole(tokens, upstream, adapter, frozen, gain_row, cosine_table, sine_table, allowed):

    def apply_section(inside, params):
        return section_apply(inside, params, frozen, gain_row, cosine_table, sine_table, allowed)

    unused, puller = jax.vjp(apply_section, tokens, adapter)
    return puller(upstream)


def keep_row(buffer, row_value, slot_index, active):
    previous = lax.dynamic_index_in_dim(buffer, slot_index, 0, keepdims=False)
    chosen = jnp.where(active, row_value, previous)
    return lax.dynamic_update_index_in_dim(buffer, chosen, slot_index, 0)


def take_row(buffer, slot_index):
    return lax.dynamic_index_in_dim(buffer, slot_index, 0, keepdims=False)


def local(
    source_tokens,
    send_counts,
    doc_segments,
    out_cotangent,
    norm_gain,
    query_weight,
    frozen_key_matrix,
    frozen_value_matrix,
    out_weight,
    adapter_down,
    adapter_up_maps,
):
    replicas = lax.axis_size("dp")
    sections = lax.axis_size("section")
    replica = lax.axis_index("dp")
    section_index = lax.axis_index("section")
    features = source_tokens.shape[1]
    slot_count = source_tokens.shape[0] // replicas
    micro_count = doc_segments.shape[0]
    token_row_count = doc_segments.shape[1]
    sent_counts = lax.dynamic_index_in_dim(send_counts, replica, 0, keepdims=False)
    send_start = jnp.cumsum(sent_counts) - sent_counts
    slot_ids = jnp.arange(slot_count, dtype=jnp.int32)
    occupied = slot_ids[None, :] < sent_counts[:, None]
    pick_rows = jnp.where(occupied, send_start[:, None] + slot_ids[None, :], 0).reshape(-1)
    packed = jnp.where(
        occupied[:, :, None],
        source_tokens[pick_rows].reshape(replicas, slot_count, features),
        jnp.zeros((), jnp.bfloat16),
    )
    arrived = lax.all_to_all(packed, "dp", split_axis=0, concat_axis=0, tiled=True)
    incoming = lax.dynamic_index_in_dim(send_counts, replica, 1, keepdims=False)
    end_rows = jnp.cumsum(incoming)
    starts = end_rows - incoming
    places = jnp.arange(micro_count * token_row_count, dtype=jnp.int32)
    source_of = jnp.minimum(
        jnp.sum((end_rows[None, :] <= places[:, None]).astype(jnp.int32), axis=1), replicas - 1
    )
    offset = places - starts[source_of]
    filled = places < end_rows[replicas - 1]
    flat_rows = jnp.where(filled, source_of * slot_count + offset, 0)
    stream = arrived.reshape(replicas * slot_count, features)[flat_rows]
    stream = jnp.where(filled[:, None], stream, jnp.zeros((), jnp.bfloat16)).reshape(
        micro_count, token_row_count, features
    )
    cosine_table, sine_table, allowed = jax.vmap(doc_layout)(
        doc_segments, filled.reshape(micro_count, token_row_count)
    )
    gathered = (
        lax.all_gather(query_weight, "dp", axis=1, tiled=True),
        lax.all_gather(frozen_key_matrix, "dp", axis=1, tiled=True),
        lax.all_gather(frozen_value_matrix, "dp", axis=1, tiled=True),
        lax.all_gather(out_weight, "dp", axis=1, tiled=True),
    )
    frozen = (gathered[0][0], gathered[1][0], gathered[2][0], gathered[3][0])
    adapter = (adapter_down[0], adapter_up_maps[0])
    gain_row = norm_gain[0]
    turn_count = micro_count + sections - 1
    zero_tokens = jnp.zeros((token_row_count, features), jnp.bfloat16)
    saved_inputs = jnp.zeros((micro_count, token_row_count, features), jnp.bfloat16)
    saved_parts = ()

    def forward_turn(turn_index, loop_state):
        inbound, kept_inputs, kept_parts = loop_state
        micro_index = turn_index - section_index
        active = (micro_index >= 0) & (micro_index < micro_count)
        slot_index = jnp.clip(micro_index, 0, micro_count - 1)
        tokens_in = jnp.where(section_index == 0, take_row(stream, slot_index), inbound)
        cos_one = take_row(cosine_table, slot_index)
        sin_one = take_row(sine_table, slot_index)
        allow_one = take_row(allowed, slot_index)
        result = lax.cond(
            active,
            lambda: section_apply(
                tokens_in, adapter, frozen, gain_row, cos_one, sin_one, allow_one
            ),
            lambda: zero_tokens,
        )
        kept_inputs = keep_row(kept_inputs, tokens_in, slot_index, active)
        inbound = from_behind(result, "section", 1)
        return (inbound, kept_inputs, kept_parts)

    forward_state = lax.fori_loop(
        0, turn_count, forward_turn, (zero_tokens, saved_inputs, saved_parts)
    )
    kept_inputs = forward_state[1]
    kept_parts = forward_state[2]
    seeds = out_cotangent.reshape(micro_count, token_row_count, features)
    zero_grads = (
        jnp.zeros(adapter[0].shape, jnp.float32),
        jnp.zeros(adapter[1].shape, jnp.float32),
    )

    def backward_turn(turn_index, loop_state):
        inbound, totals = loop_state
        micro_index = turn_index - (sections - 1 - section_index)
        active = (micro_index >= 0) & (micro_index < micro_count)
        slot_index = jnp.clip(micro_index, 0, micro_count - 1)
        upstream = jnp.where(section_index == sections - 1, take_row(seeds, slot_index), inbound)
        tokens_in = take_row(kept_inputs, slot_index)
        cos_one = take_row(cosine_table, slot_index)
        sin_one = take_row(sine_table, slot_index)
        allow_one = take_row(allowed, slot_index)

        def resting():
            return (
                zero_tokens,
                (
                    jnp.zeros(adapter[0].shape, jnp.bfloat16),
                    jnp.zeros(adapter[1].shape, jnp.bfloat16),
                ),
            )

        def compute():
            return back_whole(
                tokens_in, upstream, adapter, frozen, gain_row, cos_one, sin_one, allow_one
            )

        grad_tokens, grad_adapter = lax.cond(active, compute, resting)
        totals = (
            totals[0] + grad_adapter[0].astype(jnp.float32),
            totals[1] + grad_adapter[1].astype(jnp.float32),
        )
        inbound = from_behind(grad_tokens, "section", -1)
        return (inbound, totals)

    final_state = lax.fori_loop(0, turn_count, backward_turn, (zero_tokens, zero_grads))
    summed = lax.psum(final_state[1], "dp")
    return (summed[0][None], summed[1][None])


def solution(mesh):
    placed = (
        P("dp", None),
        P(),
        P("dp", None),
        P("dp", None),
        P("section", None),
        P("section", "dp", None),
        P("section", "dp", None),
        P("section", "dp", None),
        P("section", "dp", None),
        P("section", None, None, None),
        P("section", None, None),
    )
    return jax.shard_map(
        local,
        mesh=mesh,
        in_specs=placed,
        out_specs=(P("section", None, None, None), P("section", None, None)),
        check_vma=False,
    )
```

profile of v0, /device:TPU:6, one launch (start us, length us, event | category | flops | bytes accessed | tf_op | source)
XLA Modules:
  0.0 1809.2 jit_solution(980610044524012892)
XLA Ops:
  15.4 18.8 %all-to-all-start = ((bf16[64,4,2048]{2,1,0:T(4,128)(2,1)}), bf16[64,4,2048]{2,1,0:T(4,128)(2,1)}, u32[]{:S(2)}, u32[]{:S(2)}) async-start(bf16[64,4,2048]{2,1,0:T(4,128)(2,1)} %broadcast_select_fusion), calls=%async_computation | async-start | bytes 2097152 | tf_op jit(solution)/shard_map/all_to_all | solution.py:172
  40.5 120.8 %all-gather.9.cloned.1.call-done = bf16[1,2048,256]{2,1,0:T(8,128)(2,1)} async-done(((bf16[1,32,256]{2,1,0:T(8,128)(2,1)}), bf16[1,2048,256]{2,1,0:T(8,128)(2,1)}) %all-gather.9.cloned.1.call-update) | async-done | bytes 1048592 | tf_op jit(solution)/shard_map/all_gather | solution.py:192
  167.8 131.5 %all-gather.7.cloned.1.call-done = bf16[1,2048,256]{2,1,0:T(8,128)(2,1)} async-done(((bf16[1,32,256]{2,1,0:T(8,128)(2,1)}), bf16[1,2048,256]{2,1,0:T(8,128)(2,1)}) %all-gather.7.cloned.1.call-update) | async-done | bytes 1048592 | tf_op jit(solution)/shard_map/all_gather | solution.py:193
  299.3 144.6 %all-gather.5.cloned.1.call-done = bf16[1,1024,2048]{2,1,0:T(8,128)(2,1)} async-done(((bf16[1,16,2048]{2,1,0:T(8,128)(2,1)}), bf16[1,1024,2048]{2,1,0:T(8,128)(2,1)}) %all-gather.5.cloned.1.call-update) | async-done | bytes 4194320 | tf_op jit(solution)/shard_map/all_gather | solution.py:194
  443.9 144.0 %all-gather.11.cloned.1.call-done = bf16[1,2048,1024]{2,1,0:T(8,128)(2,1)} async-done(((bf16[1,32,1024]{2,1,0:T(8,128)(2,1)}), bf16[1,2048,1024]{2,1,0:T(8,128)(2,1)}) %all-gather.11.cloned.1.call-update) | async-done | bytes 4194320 | tf_op jit(solution)/shard_map/all_gather | solution.py:191
  588.7 271.9 %while.40 = (s32[]{:T(128)}, bf16[32,2048]{1,0:T(8,128)(2,1)S(1)}, bf16[4,32,2048]{2,1,0:T(8,128)(2,1)}, s32[]{:T(128)}, pred[]{:T(512)}, /*index=5*/bf16[4,32,2...) while((s32[]{:T(128)}, bf16[32,2048]{1,0:T(8,128)(2,1)S(1)}, ...), condition=%wide.region_9.10_spmd.clone.clone, body=%wide.region_4.9_spmd.clone.clone.sunk | while | flops 347605568 | bytes 19407876 | solution.py:224
  592.7 21.7 %conditional.9 = (bf16[32,2048]{1,0:T(8,128)(2,1)}) conditional(s32[]{:T(128)} %convert_element_type.506, () %tuple.155, (bf16[32,2048]{1,0:T(8,128)(2,1)S(1)}, f32[1,2048]{1,0:T(1,128)S(1)}, bf16[2048,256]{1,0:T(8,128)(2,1)}, bf16[2,2048,16]{1,2,0:T(8,128)(2,1)}, bf16[16,1280]{1,0:T(8,128)(2,1)}, /*index=5*/pred[32,32]{0,1:T(8,128)(4,1)S(1)}, ...), branch_computations={%region_5.5_spmd, %region_6.8_spmd} | conditional | flops 347470400 | bytes 17947588 | solution.py:213
  594.1 3.8 convolution_add_fusion.1
  610.7 3.7 fusion.12
  620.8 21.7 %conditional.9 = (bf16[32,2048]{1,0:T(8,128)(2,1)}) conditional(s32[]{:T(128)} %convert_element_type.506, () %tuple.155, (bf16[32,2048]{1,0:T(8,128)(2,1)S(1)}, f32[1,2048]{1,0:T(1,128)S(1)}, bf16[2048,256]{1,0:T(8,128)(2,1)}, bf16[2,2048,16]{1,2,0:T(8,128)(2,1)}, bf16[16,1280]{1,0:T(8,128)(2,1)}, /*index=5*/pred[32,32]{0,1:T(8,128)(4,1)S(1)}, ...), branch_computations={%region_5.5_spmd, %region_6.8_spmd} | conditional | flops 347470400 | bytes 17947588 | solution.py:213
  622.2 3.8 convolution_add_fusion.1
  638.8 3.7 fusion.12
  649.8 21.7 %conditional.9 = (bf16[32,2048]{1,0:T(8,128)(2,1)}) conditional(s32[]{:T(128)} %convert_element_type.506, () %tuple.155, (bf16[32,2048]{1,0:T(8,128)(2,1)S(1)}, f32[1,2048]{1,0:T(1,128)S(1)}, bf16[2048,256]{1,0:T(8,128)(2,1)}, bf16[2,2048,16]{1,2,0:T(8,128)(2,1)}, bf16[16,1280]{1,0:T(8,128)(2,1)}, /*index=5*/pred[32,32]{0,1:T(8,128)(4,1)S(1)}, ...), branch_computations={%region_5.5_spmd, %region_6.8_spmd} | conditional | flops 347470400 | bytes 17947588 | solution.py:213
  651.3 3.8 convolution_add_fusion.1
  667.8 3.7 fusion.12
  679.6 21.7 %conditional.9 = (bf16[32,2048]{1,0:T(8,128)(2,1)}) conditional(s32[]{:T(128)} %convert_element_type.506, () %tuple.155, (bf16[32,2048]{1,0:T(8,128)(2,1)S(1)}, f32[1,2048]{1,0:T(1,128)S(1)}, bf16[2048,256]{1,0:T(8,128)(2,1)}, bf16[2,2048,16]{1,2,0:T(8,128)(2,1)}, bf16[16,1280]{1,0:T(8,128)(2,1)}, /*index=5*/pred[32,32]{0,1:T(8,128)(4,1)S(1)}, ...), branch_computations={%region_5.5_spmd, %region_6.8_spmd} | conditional | flops 347470400 | bytes 17947588 | solution.py:213
  681.1 3.8 convolution_add_fusion.1
  697.6 3.7 fusion.12
  701.3 5.3 collective-permute-start
  712.3 26.4 %collective-permute-start = (bf16[32,2048]{1,0:T(8,128)(2,1)}, bf16[32,2048]{1,0:T(8,128)(2,1)S(1)}, u32[]{:S(2)}, u32[]{:S(2)}) collective-permute-start(bf16[32,2048]{1,0:T(8,128)(2,1)} %get-tuple-element.1925), channel_id=1, source_target_pairs={{0,64},{64,128},{128,192},{192,256},{256,320},{320,384},{384,448},... | collective-permute-start | bytes 393224 | tf_op jit(solution)/shard_map/while/body/eval_jaxpr/ppermute | solution.py:19
  744.5 5.3 collective-permute-start
  755.5 26.4 %collective-permute-start = (bf16[32,2048]{1,0:T(8,128)(2,1)}, bf16[32,2048]{1,0:T(8,128)(2,1)S(1)}, u32[]{:S(2)}, u32[]{:S(2)}) collective-permute-start(bf16[32,2048]{1,0:T(8,128)(2,1)} %get-tuple-element.1925), channel_id=1, source_target_pairs={{0,64},{64,128},{128,192},{192,256},{256,320},{320,384},{384,448},... | collective-permute-start | bytes 393224 | tf_op jit(solution)/shard_map/while/body/eval_jaxpr/ppermute | solution.py:19
  787.6 5.3 collective-permute-start
  798.7 19.9 %collective-permute-start = (bf16[32,2048]{1,0:T(8,128)(2,1)}, bf16[32,2048]{1,0:T(8,128)(2,1)S(1)}, u32[]{:S(2)}, u32[]{:S(2)}) collective-permute-start(bf16[32,2048]{1,0:T(8,128)(2,1)} %get-tuple-element.1925), channel_id=1, source_target_pairs={{0,64},{64,128},{128,192},{192,256},{256,320},{320,384},{384,448},... | collective-permute-start | bytes 393224 | tf_op jit(solution)/shard_map/while/body/eval_jaxpr/ppermute | solution.py:19
  824.3 5.3 collective-permute-start
  835.4 24.0 %collective-permute-start = (bf16[32,2048]{1,0:T(8,128)(2,1)}, bf16[32,2048]{1,0:T(8,128)(2,1)S(1)}, u32[]{:S(2)}, u32[]{:S(2)}) collective-permute-start(bf16[32,2048]{1,0:T(8,128)(2,1)} %get-tuple-element.1925), channel_id=1, source_target_pairs={{0,64},{64,128},{128,192},{192,256},{256,320},{320,384},{384,448},... | collective-permute-start | bytes 393224 | tf_op jit(solution)/shard_map/while/body/eval_jaxpr/ppermute | solution.py:19
  860.6 680.9 %while.41 = (s32[]{:T(128)}, bf16[32,2048]{1,0:T(8,128)(2,1)S(1)}, f32[2,2048,16]{1,2,0:T(8,128)}, f32[16,1280]{1,0:T(8,128)}, s32[]{:T(128)}, /*index=5*/pred[]...) while((s32[]{:T(128)}, bf16[32,2048]{1,0:T(8,128)(2,1)S(1)}, ...), condition=%wide.region_17.18_spmd.clone.clone.clone, body=%wide.region_10.17_spmd.clone.clone.clone.sunk | while | flops 569189056 | bytes 33841048 | solution.py:268
  876.9 16.9 collective-permute-done.1
  910.2 20.8 %collective-permute-done.1 = bf16[32,2048]{1,0:T(8,128)(2,1)S(1)} collective-permute-done((bf16[32,2048]{1,0:T(8,128)(2,1)S(1)}, bf16[32,2048]{1,0:T(8,128)(2,1)S(1)}, u32[]{:S(2)}, u32[]{:S(2)}) %collective-permute-start.1) | collective-permute-done | bytes 131104 | tf_op jit(solution)/shard_map/while/body/eval_jaxpr/ppermute | solution.py:19
  947.5 16.7 collective-permute-done.1
  971.6 340.0 %collective-permute-done.1 = bf16[32,2048]{1,0:T(8,128)(2,1)S(1)} collective-permute-done((bf16[32,2048]{1,0:T(8,128)(2,1)S(1)}, bf16[32,2048]{1,0:T(8,128)(2,1)S(1)}, u32[]{:S(2)}, u32[]{:S(2)}) %collective-permute-start.1) | collective-permute-done | bytes 131104 | tf_op jit(solution)/shard_map/while/body/eval_jaxpr/ppermute | solution.py:19
  1312.9 50.2 %conditional.10 = (bf16[32,2048]{1,0:T(8,128)(2,1)S(1)}, f32[2,2048,16]{1,2,0:T(8,128)}, f32[16,1280]{1,0:T(8,128)}) conditional(s32[]{:T(128)} %convert_element_type.507, () %tuple.158, (pred[]{:T(512)}, s32[]{:T(128)}, bf16[4,32,2048]{2,1,0:T(8,128)(2,1)}, bf16[32,2048]{1,0:T(8,128)(2,1)S(1)}, bf16[1024,2048]{1,0:T(8,128)(2,1)}, ...), branch_computations={%region_11.11_spmd, %region_12.16_spmd} | conditional | flops 569012928 | bytes 32267084 | solution.py:260
  1316.2 3.9 convolution_add_fusion.2
  1332.6 4.2 convolution_convert_fusion.12
  1355.3 3.5 fusion.153
  1370.8 50.2 %conditional.10 = (bf16[32,2048]{1,0:T(8,128)(2,1)S(1)}, f32[2,2048,16]{1,2,0:T(8,128)}, f32[16,1280]{1,0:T(8,128)}) conditional(s32[]{:T(128)} %convert_element_type.507, () %tuple.158, (pred[]{:T(512)}, s32[]{:T(128)}, bf16[4,32,2048]{2,1,0:T(8,128)(2,1)}, bf16[32,2048]{1,0:T(8,128)(2,1)S(1)}, bf16[1024,2048]{1,0:T(8,128)(2,1)}, ...), branch_computations={%region_11.11_spmd, %region_12.16_spmd} | conditional | flops 569012928 | bytes 32267084 | solution.py:260
  1374.1 3.9 convolution_add_fusion.2
  1390.5 4.2 convolution_convert_fusion.12
  1413.2 3.5 fusion.153
  1428.7 50.2 %conditional.10 = (bf16[32,2048]{1,0:T(8,128)(2,1)S(1)}, f32[2,2048,16]{1,2,0:T(8,128)}, f32[16,1280]{1,0:T(8,128)}) conditional(s32[]{:T(128)} %convert_element_type.507, () %tuple.158, (pred[]{:T(512)}, s32[]{:T(128)}, bf16[4,32,2048]{2,1,0:T(8,128)(2,1)}, bf16[32,2048]{1,0:T(8,128)(2,1)S(1)}, bf16[1024,2048]{1,0:T(8,128)(2,1)}, ...), branch_computations={%region_11.11_spmd, %region_12.16_spmd} | conditional | flops 569012928 | bytes 32267084 | solution.py:260
  1432.0 3.9 convolution_add_fusion.2
  1448.5 4.2 convolution_convert_fusion.12
  1471.1 3.5 fusion.153
  1486.6 50.2 %conditional.10 = (bf16[32,2048]{1,0:T(8,128)(2,1)S(1)}, f32[2,2048,16]{1,2,0:T(8,128)}, f32[16,1280]{1,0:T(8,128)}) conditional(s32[]{:T(128)} %convert_element_type.507, () %tuple.158, (pred[]{:T(512)}, s32[]{:T(128)}, bf16[4,32,2048]{2,1,0:T(8,128)(2,1)}, bf16[32,2048]{1,0:T(8,128)(2,1)S(1)}, bf16[1024,2048]{1,0:T(8,128)(2,1)}, ...), branch_computations={%region_11.11_spmd, %region_12.16_spmd} | conditional | flops 569012928 | bytes 32267084 | solution.py:260
  1489.9 3.9 convolution_add_fusion.2
  1506.4 4.2 convolution_convert_fusion.12
  1529.0 3.5 fusion.153
  1541.6 257.9 %all-reduce.11.cloned.1.call-done = (f32[1,2,2048,16]{2,3,1,0:T(8,128)}, f32[1,16,1280]{2,1,0:T(8,128)}) async-done(((f32[1,2,2048,16]{2,3,1,0:T(8,128)}, f32[1,16,1280]{2,1,0:T(8,128)}), (f32[1,2,2048,16]{2,3,1,0:T(8,128)}, f32[1,16,1280]{2,1,0:T(8,128)})) %all-reduce.11.cloned.1.call-update) | async-done | bytes 344080 | tf_op jit(solution)/shard_map/psum | solution.py:269
  (769 shorter events, 400.3 us)
Async XLA Ops:
  7.2 154.1 %all-gather.9.cloned.1.call-start = ((), (), s32[]{:S(2)}) async-start(), calls=%async_computation.3 | async-start | bytes 1064960 | tf_op jit(solution)/shard_map/all_gather | solution.py:192
  7.9 291.4 %all-gather.7.cloned.1.call-start = ((), (), s32[]{:S(2)}) async-start(), calls=%async_computation.2 | async-start | bytes 1064960 | tf_op jit(solution)/shard_map/all_gather | solution.py:193
  8.7 435.2 %all-gather.5.cloned.1.call-start = ((), (), s32[]{:S(2)}) async-start(), calls=%async_computation.1 | async-start | bytes 4259840 | tf_op jit(solution)/shard_map/all_gather | solution.py:194
  9.4 578.5 %all-gather.11.cloned.1.call-start = ((), (), s32[]{:S(2)}) async-start(), calls=%async_computation.4 | async-start | bytes 4259840 | tf_op jit(solution)/shard_map/all_gather | solution.py:191
  13.3 20.9 %copy-start.36 = (s32[64,64]{1,0:T(8,128)S(1)}, s32[64,64]{1,0:T(8,128)}, u32[]{:S(2)}) copy-start(s32[64,64]{1,0:T(8,128)} %param.20) | copy-start | bytes 49156
  15.4 147.4 %all-to-all-start = ((bf16[64,4,2048]{2,1,0:T(4,128)(2,1)}), bf16[64,4,2048]{2,1,0:T(4,128)(2,1)}, u32[]{:S(2)}, u32[]{:S(2)}) async-start(bf16[64,4,2048]{2,1,0:T(4,128)(2,1)} %broadcast_select_fusion), calls=%async_computation | async-start | bytes 2097152 | tf_op jit(solution)/shard_map/all_to_all | solution.py:172
  34.1 1765.3 %all-reduce.11.cloned.1.call-start = ((), (), s32[]{:S(2)}) async-start(), calls=%async_computation.5 | async-start | bytes 688128 | tf_op jit(solution)/shard_map/psum | solution.py:269
  162.8 425.9 %copy-start.6 = (f32[1,2048]{1,0:T(1,128)S(1)}, f32[1,2048]{1,0:T(1,128)}, u32[]{:S(2)}) copy-start(f32[1,2048]{1,0:T(1,128)} %param.23) | copy-start | bytes 24580
  594.1 12.8 copy-start.1
  614.4 2.5 collective-permute-start
  622.2 12.8 copy-start.1
  642.5 3.4 collective-permute-start
  651.3 12.8 copy-start.1
  671.5 4.2 collective-permute-start
  681.0 12.8 copy-start.1
  701.3 6.5 collective-permute-start
  712.3 27.5 %collective-permute-start = (bf16[32,2048]{1,0:T(8,128)(2,1)}, bf16[32,2048]{1,0:T(8,128)(2,1)S(1)}, u32[]{:S(2)}, u32[]{:S(2)}) collective-permute-start(bf16[32,2048]{1,0:T(8,128)(2,1)} %get-tuple-element.1925), channel_id=1, source_target_pairs={{0,64},{64,128},{128,192},{192,256},{256,320},{320,384},{384,448},... | collective-permute-start | bytes 393224 | tf_op jit(solution)/shard_map/while/body/eval_jaxpr/ppermute | solution.py:19
  744.5 6.5 collective-permute-start
  755.5 27.5 %collective-permute-start = (bf16[32,2048]{1,0:T(8,128)(2,1)}, bf16[32,2048]{1,0:T(8,128)(2,1)S(1)}, u32[]{:S(2)}, u32[]{:S(2)}) collective-permute-start(bf16[32,2048]{1,0:T(8,128)(2,1)} %get-tuple-element.1925), channel_id=1, source_target_pairs={{0,64},{64,128},{128,192},{192,256},{256,320},{320,384},{384,448},... | collective-permute-start | bytes 393224 | tf_op jit(solution)/shard_map/while/body/eval_jaxpr/ppermute | solution.py:19
  787.6 6.5 collective-permute-start
  798.7 21.1 %collective-permute-start = (bf16[32,2048]{1,0:T(8,128)(2,1)}, bf16[32,2048]{1,0:T(8,128)(2,1)S(1)}, u32[]{:S(2)}, u32[]{:S(2)}) collective-permute-start(bf16[32,2048]{1,0:T(8,128)(2,1)} %get-tuple-element.1925), channel_id=1, source_target_pairs={{0,64},{64,128},{128,192},{192,256},{256,320},{320,384},{384,448},... | collective-permute-start | bytes 393224 | tf_op jit(solution)/shard_map/while/body/eval_jaxpr/ppermute | solution.py:19
  824.3 6.5 collective-permute-start
  835.4 25.2 %collective-permute-start = (bf16[32,2048]{1,0:T(8,128)(2,1)}, bf16[32,2048]{1,0:T(8,128)(2,1)S(1)}, u32[]{:S(2)}, u32[]{:S(2)}) collective-permute-start(bf16[32,2048]{1,0:T(8,128)(2,1)} %get-tuple-element.1925), channel_id=1, source_target_pairs={{0,64},{64,128},{128,192},{192,256},{256,320},{320,384},{384,448},... | collective-permute-start | bytes 393224 | tf_op jit(solution)/shard_map/while/body/eval_jaxpr/ppermute | solution.py:19
  863.4 6.1 collective-permute-start.1
  872.3 21.5 %collective-permute-start.1 = (bf16[32,2048]{1,0:T(8,128)(2,1)S(1)}, bf16[32,2048]{1,0:T(8,128)(2,1)S(1)}, u32[]{:S(2)}, u32[]{:S(2)}) collective-permute-start(bf16[32,2048]{1,0:T(8,128)(2,1)S(1)} %get-tuple-element.1771), channel_id=1, source_target_pairs={{64,0},{128,64},{192,128},{256,192},{320,256},{384,320},{448,384},... | collective-permute-start | bytes 393224 | tf_op jit(solution)/shard_map/while/body/eval_jaxpr/ppermute | solution.py:19
  896.5 6.3 collective-permute-start.1
  905.6 25.5 %collective-permute-start.1 = (bf16[32,2048]{1,0:T(8,128)(2,1)S(1)}, bf16[32,2048]{1,0:T(8,128)(2,1)S(1)}, u32[]{:S(2)}, u32[]{:S(2)}) collective-permute-start(bf16[32,2048]{1,0:T(8,128)(2,1)S(1)} %get-tuple-element.1771), channel_id=1, source_target_pairs={{64,0},{128,64},{192,128},{256,192},{320,256},{384,320},{448,384},... | collective-permute-start | bytes 393224 | tf_op jit(solution)/shard_map/while/body/eval_jaxpr/ppermute | solution.py:19
  933.8 6.3 collective-permute-start.1
  942.8 21.4 %collective-permute-start.1 = (bf16[32,2048]{1,0:T(8,128)(2,1)S(1)}, bf16[32,2048]{1,0:T(8,128)(2,1)S(1)}, u32[]{:S(2)}, u32[]{:S(2)}) collective-permute-start(bf16[32,2048]{1,0:T(8,128)(2,1)S(1)} %get-tuple-element.1771), channel_id=1, source_target_pairs={{64,0},{128,64},{192,128},{256,192},{320,256},{384,320},{448,384},... | collective-permute-start | bytes 393224 | tf_op jit(solution)/shard_map/while/body/eval_jaxpr/ppermute | solution.py:19
  966.9 344.6 %collective-permute-start.1 = (bf16[32,2048]{1,0:T(8,128)(2,1)S(1)}, bf16[32,2048]{1,0:T(8,128)(2,1)S(1)}, u32[]{:S(2)}, u32[]{:S(2)}) collective-permute-start(bf16[32,2048]{1,0:T(8,128)(2,1)S(1)} %get-tuple-element.1771), channel_id=1, source_target_pairs={{64,0},{128,64},{192,128},{256,192},{320,256},{384,320},{448,384},... | collective-permute-start | bytes 393224 | tf_op jit(solution)/shard_map/while/body/eval_jaxpr/ppermute | solution.py:19
  1312.9 19.7 %copy-start.4 = (bf16[32,2048]{1,0:T(8,128)(2,1)}, bf16[32,2048]{1,0:T(8,128)(2,1)S(1)}, u32[]{:S(2)}) copy-start(bf16[32,2048]{1,0:T(8,128)(2,1)S(1)} %get-tuple-element.946) | copy-start | bytes 393220 | tf_op jit(solution)/shard_map/while/body/eval_jaxpr/cond
  1316.2 12.3 copy-start.2
  1326.6 14.3 copy-start.3
  1342.5 9.8 copy-start.13
  1363.2 6.3 collective-permute-start.1
  1370.8 19.7 %copy-start.4 = (bf16[32,2048]{1,0:T(8,128)(2,1)}, bf16[32,2048]{1,0:T(8,128)(2,1)S(1)}, u32[]{:S(2)}) copy-start(bf16[32,2048]{1,0:T(8,128)(2,1)S(1)} %get-tuple-element.946) | copy-start | bytes 393220 | tf_op jit(solution)/shard_map/while/body/eval_jaxpr/cond
  1374.1 12.3 copy-start.2
  1384.5 14.3 copy-start.3
  1400.4 9.8 copy-start.13
  1421.1 6.3 collective-permute-start.1
  1428.7 19.7 %copy-start.4 = (bf16[32,2048]{1,0:T(8,128)(2,1)}, bf16[32,2048]{1,0:T(8,128)(2,1)S(1)}, u32[]{:S(2)}) copy-start(bf16[32,2048]{1,0:T(8,128)(2,1)S(1)} %get-tuple-element.946) | copy-start | bytes 393220 | tf_op jit(solution)/shard_map/while/body/eval_jaxpr/cond
  1432.0 12.3 copy-start.2
  1442.4 14.3 copy-start.3
  1479.0 6.3 collective-permute-start.1
  1486.6 19.7 %copy-start.4 = (bf16[32,2048]{1,0:T(8,128)(2,1)}, bf16[32,2048]{1,0:T(8,128)(2,1)S(1)}, u32[]{:S(2)}) copy-start(bf16[32,2048]{1,0:T(8,128)(2,1)S(1)} %get-tuple-element.946) | copy-start | bytes 393220 | tf_op jit(solution)/shard_map/while/body/eval_jaxpr/cond
  1489.9 12.3 copy-start.2
  1500.3 14.3 copy-start.3
  1536.9 4.6 collective-permute-start.1
  (123 other events, 392.9 us)
Sparse Core Ops, SparseCore 0:
  11.0 150.2 all-gather.8
  164.2 134.9 all-gather.6
  302.2 141.5 all-gather.4
  446.7 141.1 all-gather.10
  1541.7 257.7 all-reduce.10
where the time goes:
time: 1820 us; the launch traced here: 1810 us
  waiting for transfers between devices  1220 us (67%)
  matrix products  201 us (11%)
  starting transfers between devices  157 us (9%)
  other arithmetic  128 us (7%)
  local copies, waits for them, and re-layouts  87.3 us (5%)
    ppermute x22, waiting for transfers between devices, from_behind(): return lax.ppermute(block, axis, route)  417 us
    psum x1, waiting for transfers between devices, local(): summed = lax.psum(final_state[1], 'dp')  258 us
    all_gather x1, waiting for transfers between devices, local(): lax.all_gather(out_weight, 'dp', axis=1, tiled=True)  145 us
    all_gather x1, waiting for transfers between devices, local(): lax.all_gather(query_weight, 'dp', axis=1, tiled=True)  144 us
    ppermute x22, starting transfers between devices, from_behind(): return lax.ppermute(block, axis, route)  139 us
    all_gather x1, waiting for transfers between devices, local(): lax.all_gather(frozen_value_matrix, 'dp', axis=1, tiled=True)  131 us
    all_gather x1, waiting for transfers between devices, local(): lax.all_gather(frozen_key_matrix, 'dp', axis=1, tiled=True)  121 us
    dot_general x12, matrix products, project(): jnp.dot(normed_hidden, w_query, preferred_element_type=jnp.float32)  44.8 us
  transfers between devices with their start and end apart: 28, of which 26 were waited for; matrix products, arithmetic and copies ran while one was open for 3% of the time, Pallas kernels for 0%

commit v1 on v0

v1 whole, which is shorter than its diff:
```python
import functools

import jax
import jax.numpy as jnp
from jax import lax
from jax.experimental import pallas as pl
from jax.experimental.pallas import tpu as pltpu
from jax.sharding import PartitionSpec as P

QUERY_HEADS = 16
KEY_VALUE_HEADS = 4
GROUP = QUERY_HEADS // KEY_VALUE_HEADS
HEAD_SIZE = 64
QUERY_WIDTH = QUERY_HEADS * HEAD_SIZE
KEY_WIDTH = KEY_VALUE_HEADS * HEAD_SIZE
RANK = 16
LANES = 128

ROPE_BASE = 500000.0
ADAPTER_SCALE = 2.0
NORM_EPS = 1e-05
SCORE_SCALE = HEAD_SIZE ** (-0.5)

X_CHIPS = 4

F32 = jnp.float32
BF16 = jnp.bfloat16
VMEM_LIMIT = 40 * 1024 * 1024


def dot(a, b):
    return jnp.dot(a, b, preferred_element_type=F32)


def dot_nt(a, b):
    return lax.dot_general(a, b, (((1,), (1,)), ((), ())), preferred_element_type=F32)


def dot_tn(a, b):
    return lax.dot_general(a, b, (((0,), (0,)), ((), ())), preferred_element_type=F32)


def lanes_of(rows, width):
    return lax.broadcasted_iota(jnp.int32, (rows, width), 1)


def rope(t, cosine, signed_sine):
    rows, width = t.shape
    copies = width // LANES
    wide_cos = jnp.concatenate([cosine] * copies, axis=1)
    wide_sin = jnp.concatenate([signed_sine] * copies, axis=1)
    half = HEAD_SIZE // 2
    leading = (lanes_of(rows, width) % HEAD_SIZE) < half
    partner = jnp.where(leading, pltpu.roll(t, width - half, 1), pltpu.roll(t, half, 1))
    return t * wide_cos + partner * wide_sin


def expand(turned, head):
    rows, width = turned[0].shape
    block = lanes_of(rows, width) // HEAD_SIZE
    zero = jnp.zeros((), turned[0].dtype)
    parts = [
        jnp.where(block == g, turned[(g - head) % KEY_VALUE_HEADS], zero) for g in range(GROUP)
    ]
    return jnp.concatenate(parts, axis=0)


def turns_of(t):
    width = t.shape[1]
    wide = t.astype(F32)
    return [t] + [
        pltpu.roll(wide, j * HEAD_SIZE, 1).astype(t.dtype) for j in range(1, KEY_VALUE_HEADS)
    ]


def fold(products):
    rows = products[0].shape[0] // GROUP
    width = products[0].shape[1]
    block = lanes_of(rows, width) // HEAD_SIZE
    total = None
    for h, product in enumerate(products):
        diagonal = None
        for g in range(GROUP):
            part = jnp.where(block == g, product[g * rows : (g + 1) * rows], 0.0)
            diagonal = part if diagonal is None else diagonal + part
        pair = diagonal + pltpu.roll(diagonal, HEAD_SIZE, 1)
        whole = pair + pltpu.roll(pair, 2 * HEAD_SIZE, 1)
        kept = jnp.where(block == h, whole, 0.0)
        total = kept if total is None else total + kept
    return total


def forward_kernel(
    x_ref, gain_ref, wqkv_ref, wout_ref, down_ref, upq_ref, upv_ref, cos_ref, sin_ref, mask_ref,
    y_ref, q_ref, k_ref, v_ref, p_ref, low_ref, n_ref,
):
    hidden = x_ref[...].astype(F32)
    energy = jnp.mean(hidden * hidden, axis=-1, keepdims=True)
    n = (hidden * lax.rsqrt(energy + NORM_EPS) * gain_ref[...]).astype(BF16)
    n_ref[...] = n
    cosine, sine = cos_ref[...], sin_ref[...]
    low = dot(n, down_ref[...]).astype(BF16)
    low_ref[...] = low
    k = rope(dot(n, wqkv_ref[:, QUERY_WIDTH : QUERY_WIDTH + KEY_WIDTH]), cosine, sine).astype(BF16)
    k_ref[...] = k
    v = dot(n, wqkv_ref[:, QUERY_WIDTH + KEY_WIDTH :]) + ADAPTER_SCALE * dot(low, upv_ref[...])
    v = v.astype(BF16)
    v_ref[...] = v
    k_turns, v_turns = turns_of(k), turns_of(v)
    allowed = mask_ref[...] > 0.0
    tokens = hidden.shape[0]
    width = GROUP * HEAD_SIZE
    blended = []
    for h in range(KEY_VALUE_HEADS):
        at = slice(h * width, (h + 1) * width)
        q = dot(n, wqkv_ref[:, at]) + ADAPTER_SCALE * dot(low, upq_ref[:, at])
        q = rope(q, cosine, sine).astype(BF16)
        q_ref[:, at] = q
        scores = dot_nt(q, expand(k_turns, h)) * SCORE_SCALE
        shares = []
        for g in range(GROUP):
            weights = jnp.where(allowed, jnp.exp(scores[:, g * tokens : (g + 1) * tokens]), 0.0)
            shares.append((weights / jnp.sum(weights, axis=-1, keepdims=True)).astype(BF16))
        shares = jnp.concatenate(shares, axis=1)
        p_ref[:, h * GROUP * tokens : (h + 1) * GROUP * tokens] = shares
        blended.append(dot(shares, expand(v_turns, h)).astype(BF16))
    blended = jnp.concatenate(blended, axis=1)
    y_ref[...] = (hidden + dot(blended, wout_ref[...])).astype(BF16)


def backward_kernel(
    c_ref, x_ref, gain_ref, wqkv_ref, wout_ref, down_ref, upq_ref, upv_ref, cos_ref, sin_ref,
    q_ref, k_ref, v_ref, p_ref,
    out_ref, dq_ref, dv_ref, dlow_ref,
):
    c = c_ref[...]
    tokens = c.shape[0]
    width = GROUP * HEAD_SIZE
    cosine, sine = cos_ref[...], sin_ref[...]
    k_turns, v_turns = turns_of(k_ref[...]), turns_of(v_ref[...])
    dn = None
    dlow = None
    dk_products, dv_products = [], []
    for h in range(KEY_VALUE_HEADS):
        at = slice(h * width, (h + 1) * width)
        dblended = dot_nt(c, wout_ref[at, :]).astype(BF16)
        shares = p_ref[:, h * GROUP * tokens : (h + 1) * GROUP * tokens]
        dshares = dot_nt(dblended, expand(v_turns, h))
        dscores = []
        for g in range(GROUP):
            span = slice(g * tokens, (g + 1) * tokens)
            p = shares[:, span].astype(F32)
            dp = dshares[:, span]
            pdp = p * dp
            dscores.append(
                ((pdp - p * jnp.sum(pdp, axis=-1, keepdims=True)) * SCORE_SCALE).astype(BF16)
            )
        dscores = jnp.concatenate(dscores, axis=1)
        dq = dot(dscores, expand(k_turns, h))
        dq = rope(dq, cosine, -sine).astype(BF16)
        dq_ref[:, at] = dq
        part = dot_nt(dq, upq_ref[:, at])
        dlow = part if dlow is None else dlow + part
        part = dot_nt(dq, wqkv_ref[:, at])
        dn = part if dn is None else dn + part
        dv_products.append(dot_tn(shares, dblended))
        dk_products.append(dot_tn(dscores, q_ref[:, at]))
    dk = rope(fold(dk_products), cosine, -sine).astype(BF16)
    dv = fold(dv_products).astype(BF16)
    dv_ref[...] = dv
    dlow = (ADAPTER_SCALE * (dlow + dot_nt(dv, upv_ref[...]))).astype(BF16)
    dlow_ref[...] = dlow
    dn = dn + dot_nt(dk, wqkv_ref[:, QUERY_WIDTH : QUERY_WIDTH + KEY_WIDTH])
    dn = dn + dot_nt(dv, wqkv_ref[:, QUERY_WIDTH + KEY_WIDTH :])
    dn = dn + dot_nt(dlow, down_ref[...])
    hidden = x_ref[...].astype(F32)
    energy = jnp.mean(hidden * hidden, axis=-1, keepdims=True)
    scale = lax.rsqrt(energy + NORM_EPS)
    dy = dn * gain_ref[...]
    along = jnp.mean(hidden * dy, axis=-1, keepdims=True)
    dh = scale * dy - hidden * (scale * scale * scale * along)
    out_ref[...] = (c.astype(F32) + dh).astype(BF16)


def grads_kernel(n_ref, low_ref, dq_ref, dv_ref, dlow_ref, g_ref):
    g_ref[...] = jnp.zeros_like(g_ref)
    g_ref[0 : 2 * RANK, :] = dot_tn(dlow_ref[...], n_ref[...])[: 2 * RANK]
    low = low_ref[...]
    up_q = ADAPTER_SCALE * dot_tn(low, dq_ref[...])
    up_v = ADAPTER_SCALE * dot_tn(low, dv_ref[...])
    g_ref[2 * RANK : 3 * RANK, 0:QUERY_WIDTH] = up_q[:RANK]
    g_ref[2 * RANK : 3 * RANK, QUERY_WIDTH : QUERY_WIDTH + KEY_WIDTH] = up_v[RANK : 2 * RANK]


def call(kernel, outs, *args):
    return pl.pallas_call(
        kernel,
        out_shape=[jax.ShapeDtypeStruct(shape, dtype) for shape, dtype in outs],
        in_specs=[pl.BlockSpec(memory_space=pltpu.VMEM)] * len(args),
        out_specs=[pl.BlockSpec(memory_space=pltpu.VMEM)] * len(outs),
        compiler_params=pltpu.CompilerParams(vmem_limit_bytes=VMEM_LIMIT),
    )(*args)


def z_route(replicas, distance):
    return [(i, (i + distance * X_CHIPS) % replicas) for i in range(replicas)]


def x_route(replicas, distance):
    return [
        (i, i // X_CHIPS * X_CHIPS + (i % X_CHIPS + distance) % X_CHIPS) for i in range(replicas)
    ]


def ring(piece, route, count, place, put, split):
    put(place, None, piece)
    ahead = behind = piece
    for step in range(1, count // 2):
        ahead = lax.ppermute(ahead, "dp", route(1))
        behind = lax.ppermute(behind, "dp", route(-1))
        put((place - step) % count, None, ahead)
        put((place + step) % count, None, behind)
    step = count // 2
    ahead = lax.ppermute(split(ahead)[0], "dp", route(1))
    behind = lax.ppermute(split(behind)[1], "dp", route(-1))
    put((place - step) % count, 0, ahead)
    put((place + step) % count, 1, behind)


def gather_weights(shard, replica, replicas):
    rows, columns = shard.shape
    z_count = replicas // X_CHIPS
    z, x = replica // X_CHIPS, replica % X_CHIPS
    line = [jnp.zeros((X_CHIPS, rows, columns), shard.dtype)]

    def put_line(at, part, data):
        start = rows // 2 if part == 1 else 0
        line[0] = lax.dynamic_update_slice(line[0], data[None], (at, start, 0))

    ring(
        shard,
        functools.partial(x_route, replicas),
        X_CHIPS,
        x,
        put_line,
        lambda t: (t[: rows // 2], t[rows // 2 :]),
    )
    qkv_width = QUERY_WIDTH + 2 * KEY_WIDTH
    half = rows // 2
    qkv = [jnp.zeros((z_count, X_CHIPS, rows, qkv_width), shard.dtype)]
    out = [jnp.zeros((z_count, X_CHIPS, half, 2 * QUERY_WIDTH), shard.dtype)]

    def put_plane(at, part, data):
        start = X_CHIPS // 2 if part == 1 else 0
        qkv[0] = lax.dynamic_update_slice(qkv[0], data[None, :, :, :qkv_width], (at, start, 0, 0))
        left = data[None, :, :half, qkv_width:]
        right = data[None, :, half:, qkv_width:]
        out[0] = lax.dynamic_update_slice(
            out[0], jnp.concatenate([left, right], axis=-1), (at, start, 0, 0)
        )

    ring(
        line[0],
        functools.partial(z_route, replicas),
        z_count,
        z,
        put_plane,
        lambda t: (t[: X_CHIPS // 2], t[X_CHIPS // 2 :]),
    )
    return (
        qkv[0].reshape(replicas * rows, qkv_width),
        out[0].reshape(replicas * half, 2 * QUERY_WIDTH),
    )


def sum_over_replicas(grads, replica, replicas):
    rows, columns = grads.shape
    z_count = replicas // X_CHIPS
    x = replica % X_CHIPS
    part_width = columns // X_CHIPS
    parts = grads.reshape(rows, X_CHIPS, part_width).transpose(1, 0, 2)
    sent = parts.astype(BF16)
    total = lax.dynamic_index_in_dim(parts, x, 0, keepdims=False)
    for distance in range(1, X_CHIPS):
        piece = lax.dynamic_index_in_dim(sent, (x + distance) % X_CHIPS, 0, keepdims=False)
        total = total + lax.ppermute(piece, "dp", x_route(replicas, distance)).astype(F32)
    low_count = 4
    sent = total.astype(BF16)
    for distance in range(1, low_count):
        route = []
        for i in range(replicas):
            zi, xi = i // X_CHIPS, i % X_CHIPS
            to = zi // low_count * low_count + (zi % low_count + distance) % low_count
            route.append((i, to * X_CHIPS + xi))
        total = total + lax.ppermute(sent, "dp", route).astype(F32)
    sent = total.astype(BF16)
    for distance in range(1, z_count // low_count):
        route = z_route(replicas, distance * low_count)
        total = total + lax.ppermute(sent, "dp", route).astype(F32)
    sent = total.astype(BF16)
    whole = jnp.zeros((X_CHIPS, rows, part_width), F32)
    whole = lax.dynamic_update_slice(whole, total[None], (x, 0, 0))
    for distance in range(1, X_CHIPS):
        piece = lax.ppermute(sent, "dp", x_route(replicas, distance)).astype(F32)
        whole = lax.dynamic_update_slice(whole, piece[None], ((x - distance) % X_CHIPS, 0, 0))
    return whole.transpose(1, 0, 2).reshape(rows, columns)


def exchange_tokens(source_tokens, send_counts, replica, replicas, stream_count):
    slot_count = source_tokens.shape[0] // replicas
    features = source_tokens.shape[1]
    sent_counts = lax.dynamic_index_in_dim(send_counts, replica, 0, keepdims=False)
    send_start = jnp.cumsum(sent_counts) - sent_counts
    slot_ids = jnp.arange(slot_count, dtype=jnp.int32)
    occupied = slot_ids[None, :] < sent_counts[:, None]
    pick_rows = jnp.where(occupied, send_start[:, None] + slot_ids[None, :], -1).reshape(-1)
    own_rows = jnp.arange(source_tokens.shape[0], dtype=jnp.int32)
    choose = (pick_rows[:, None] == own_rows[None, :]).astype(BF16)
    packed = dot(choose, source_tokens).astype(BF16).reshape(replicas, slot_count, features)
    arrived = lax.all_to_all(packed, "dp", split_axis=0, concat_axis=0, tiled=True)
    incoming = lax.dynamic_index_in_dim(send_counts, replica, 1, keepdims=False)
    end_rows = jnp.cumsum(incoming)
    starts = end_rows - incoming
    places = jnp.arange(stream_count, dtype=jnp.int32)
    slot_place = starts[:, None] + slot_ids[None, :]
    slot_place = jnp.where(slot_ids[None, :] < incoming[:, None], slot_place, -1).reshape(-1)
    choose = (places[:, None] == slot_place[None, :]).astype(BF16)
    stream = dot(choose, arrived.reshape(replicas * slot_count, features)).astype(BF16)
    return stream, places < end_rows[replicas - 1]


def layout(segments, filled):
    micro_count, token_count = segments.shape
    tokens = micro_count * token_count
    segment = segments.reshape(tokens)
    places = jnp.arange(tokens, dtype=jnp.int32)
    sequence = places // token_count
    same = (segment[:, None] == segment[None, :]) & (sequence[:, None] == sequence[None, :])
    before = places[None, :] < places[:, None]
    position = jnp.sum(jnp.where(same & before, 1.0, 0.0).astype(F32), axis=1)
    alone = places[None, :] == places[:, None]
    allowed = (before & same & filled[:, None] & filled[None, :]) | alone
    half = HEAD_SIZE // 2
    frequency = ROPE_BASE ** (-2.0 * jnp.arange(half, dtype=F32) / HEAD_SIZE)
    angles = position[:, None] * frequency[None, :]
    cosine, sine = jnp.cos(angles), jnp.sin(angles)
    heads = LANES // HEAD_SIZE
    return (
        jnp.concatenate([cosine, cosine] * heads, axis=1),
        jnp.concatenate([-sine, sine] * heads, axis=1),
        allowed.astype(F32),
    )


def local(
    source_tokens,
    send_counts,
    doc_segments,
    out_cotangent,
    norm_gain,
    query_weight,
    frozen_key_matrix,
    frozen_value_matrix,
    out_weight,
    adapter_down,
    adapter_up_maps,
):
    replicas = lax.axis_size("dp")
    sections = lax.axis_size("section")
    replica = lax.axis_index("dp")
    section = lax.axis_index("section")
    features = source_tokens.shape[1]
    tokens = doc_segments.shape[0] * doc_segments.shape[1]

    half = out_weight.shape[2] // 2
    out_rows = jnp.concatenate([out_weight[0, :, :half], out_weight[0, :, half:]], axis=0)
    shard = jnp.concatenate(
        [query_weight[0], frozen_key_matrix[0], frozen_value_matrix[0], out_rows], axis=1
    )
    stream, filled = exchange_tokens(source_tokens, send_counts, replica, replicas, tokens)
    cosine, sine, allowed = layout(doc_segments, filled)
    wqkv, wout = gather_weights(shard, replica, replicas)
    gain = norm_gain[0].reshape(1, features)
    spare = LANES - 2 * RANK
    down = jnp.concatenate(
        [adapter_down[0, 0], adapter_down[0, 1], jnp.zeros((features, spare), BF16)], axis=1
    )
    up = adapter_up_maps[0]
    up_q = jnp.concatenate([up[:, :QUERY_WIDTH], jnp.zeros((LANES - RANK, QUERY_WIDTH), BF16)])
    up_v = jnp.concatenate(
        [
            jnp.zeros((RANK, KEY_WIDTH), BF16),
            up[:, QUERY_WIDTH:],
            jnp.zeros((spare, KEY_WIDTH), BF16),
        ]
    )

    saved_shapes = [
        ((tokens, QUERY_WIDTH), BF16),
        ((tokens, KEY_WIDTH), BF16),
        ((tokens, KEY_WIDTH), BF16),
        ((tokens, QUERY_HEADS * tokens), BF16),
        ((tokens, LANES), BF16),
        ((tokens, features), BF16),
    ]
    x = stream
    saved = tuple(jnp.zeros(shape, dtype) for shape, dtype in saved_shapes)
    for turn in range(sections):

        def run(x, saved):
            made = call(
                forward_kernel,
                [((tokens, features), BF16)] + saved_shapes,
                x, gain, wqkv, wout, down, up_q, up_v, cosine, sine, allowed,
            )
            return made[0], tuple(made[1:])

        y, saved = lax.cond(section == turn, run, lambda x, saved: (x, saved), x, saved)
        if turn + 1 < sections:
            came = lax.ppermute(y, "section", [(turn, turn + 1)])
            x = jnp.where(section == turn + 1, came, x)

    q, k, v, shares, low, normed = saved
    c = out_cotangent
    kept = (
        jnp.zeros((tokens, QUERY_WIDTH), BF16),
        jnp.zeros((tokens, KEY_WIDTH), BF16),
        jnp.zeros((tokens, LANES), BF16),
    )
    for turn in range(sections - 1, -1, -1):

        def run_back(c, kept):
            made = call(
                backward_kernel,
                [((tokens, features), BF16)] + [(t.shape, t.dtype) for t in kept],
                c, x, gain, wqkv, wout, down, up_q, up_v, cosine, sine, q, k, v, shares,
            )
            return made[0], tuple(made[1:])

        back, kept = lax.cond(section == turn, run_back, lambda c, kept: (c, kept), c, kept)
        if turn > 0:
            came = lax.ppermute(back, "section", [(turn, turn - 1)])
            c = jnp.where(section == turn - 1, came, c)

    (grads,) = call(
        grads_kernel, [((3 * RANK, features), F32)], normed, low, kept[0], kept[1], kept[2]
    )
    grads = sum_over_replicas(grads, replica, replicas)
    down_grads = grads[: 2 * RANK].reshape(2, RANK, features).transpose(0, 2, 1)
    up_grads = grads[2 * RANK :, : QUERY_WIDTH + KEY_WIDTH]
    return (down_grads[None], up_grads[None])


def solution(mesh):
    placed = (
        P("dp", None),
        P(),
        P("dp", None),
        P("dp", None),
        P("section", None),
        P("section", "dp", None),
        P("section", "dp", None),
        P("section", "dp", None),
        P("section", "dp", None),
        P("section", None, None, None),
        P("section", None, None),
    )
    return jax.shard_map(
        local,
        mesh=mesh,
        in_specs=placed,
        out_specs=(P("section", None, None, None), P("section", None, None)),
        check_vma=False,
    )
```

time: 1820 us -> 553 us (0.30)
  waiting for transfers between devices: 1220 us -> 277 us
  matrix products: 201 us -> 0.8 us
  other arithmetic: 128 us -> 22.7 us
  local copies, waits for them, and re-layouts: 87.3 us -> 53.1 us
  Pallas kernels: 0 us -> 22.5 us
    all_gather x4 -> x0, waiting for transfers between devices: 541 us -> none  [the longest x1 145 us: local(): lax.all_gather(out_weight, 'dp', axis=1, tiled=True)]
    psum x1 -> x0, waiting for transfers between devices: 258 us -> none  [local(): summed = lax.psum(final_state[1], 'dp')]
    dot_general x128 -> x2, matrix products: 201 us -> 0.8 us  [dot(): return jnp.dot(a, b, preferred_element_type=F32)]
    ppermute x22 -> x46, waiting for transfers between devices: 417 us -> 277 us  [the longest x7 192 us: local(): came = lax.ppermute(back, 'section', [(turn, turn - 1)])]
    add x22 -> x0, other arithmetic: 36.6 us -> none  [the longest x11 19.4 us: backward_turn(): totals[0] + grad_adapter[0].astype(jnp.float32)]
    mul x22 -> x0, other arithmetic: 30.2 us -> none  [doc_layout(): angles = position[:, None] * frequency[None, :]]
    pallas_call x0 -> x3, Pallas kernels: none -> 22.5 us  [call(): pl.pallas_call(kernel, out_shape=[jax.ShapeDtypeStruct(shape, dtype) for...]
    dynamic_slice x28 -> x1, local copies, waits for them, and re-layouts: 22.4 us -> 0.08 us  [exchange_tokens(): incoming = lax.dynamic_index_in_dim(send_counts, replica, 1, keepdims=False)]
  transfers between devices with their start and end apart: 28 -> 47, of which waited for: 26 -> 20; matrix products, arithmetic and copies ran while one was open for 3% -> 9% of each run, Pallas kernels for 0% -> 0%
where the time goes in v1:
time: 553 us; the launch traced here: 544 us
  waiting for transfers between devices  277 us (50%)
  starting transfers between devices  149 us (27%)
  local copies, waits for them, and re-layouts  53.1 us (10%)
  other arithmetic  22.7 us (4%)
  Pallas kernels  22.5 us (4%)
  loops' own time  16.2 us (3%)
    ppermute x7, waiting for transfers between devices, local(): came = lax.ppermute(back, 'section', [(turn, turn - 1)])  192 us
    ppermute x8, waiting for transfers between devices, ring(): ahead = lax.ppermute(ahead, 'dp', route(1))  59.3 us
    ppermute x8, starting transfers between devices, ring(): behind = lax.ppermute(behind, 'dp', route(-1))  37.1 us
    ppermute x6, starting transfers between devices, sum_over_replicas(): total = total + lax.ppermute(sent, 'dp', route).astype(F32)  29.6 us
    pallas_call x3, Pallas kernels, call(): pl.pallas_call(kernel, out_shape=[jax.ShapeDtypeStruct(shape, dtype) for...  22.5 us
    ppermute x8, starting transfers between devices, ring(): ahead = lax.ppermute(ahead, 'dp', route(1))  22.4 us
    dynamic_update_slice x17, local copies, waits for them, and re-layouts, put_plane(): lax.dynamic_update_slice(qkv[0], data[None, :, :, :qkv_width], (at, start...  17.1 us
    all_to_all x1, starting transfers between devices, exchange_tokens(): lax.all_to_all(packed, 'dp', split_axis=0, concat_axis=0, tiled=True)  14.7 us
  transfers between devices with their start and end apart: 47, of which 20 were waited for; matrix products, arithmetic and copies ran while one was open for 9% of the time, Pallas kernels for 0%

profile of v1, /device:TPU:6, one launch (start us, length us, event | category | flops | bytes accessed | tf_op | source)
XLA Modules:
  0.0 544.0 jit_solution(10879801284518497153)
XLA Ops:
  3.1 7.7 %collective-permute-start = (bf16[32,2560]{1,0:T(8,128)(2,1)}, bf16[32,2560]{1,0:T(8,128)(2,1)S(1)}, u32[]{:S(2)}, u32[]{:S(2)}) collective-permute-start(bf16[32,2560]{1,0:T(8,128)(2,1)} %maximum_maximum_fusion.1), channel_id=1, source_target_pairs={{0,1},{1,2},{2,3},{3,0},{4,5},{5,6},{6,7},{7,4},{8,9},{9,10},{10,1... | collective-permute-start | bytes 491528 | tf_op jit(solution)/shard_map/ppermute | solution.py:219
  10.9 1.9 collective-permute-start.1
  16.5 14.7 %all-to-all-start = ((bf16[64,4,2048]{2,1,0:T(4,128)(2,1)}), bf16[64,4,2048]{2,1,0:T(4,128)(2,1)S(1)}, u32[]{:S(2)}, u32[]{:S(2)}) async-start(bf16[64,4,2048]{2,1,0:T(4,128)(2,1)} %reshape.177), calls=%async_computation | async-start | bytes 2097152 | tf_op jit(solution)/shard_map/all_to_all | solution.py:320
  37.9 2.4 collective-permute-start.2
  41.2 3.5 collective-permute-start.3
  45.6 3.4 collective-permute-done.3
  49.0 3.2 collective-permute-start.4
  52.3 3.9 collective-permute-start.5
  56.1 3.4 broadcast_in_dim.252
  60.3 2.5 broadcast_in_dim.276
  63.5 29.1 %collective-permute-done.4 = bf16[4,32,2560]{2,1,0:T(8,128)(2,1)S(1)} collective-permute-done((bf16[4,32,2560]{2,1,0:T(8,128)(2,1)S(1)}, bf16[4,32,2560]{2,1,0:T(8,128)(2,1)S(1)}, u32[]{:S(2)}, u32[]{:S(2)}) %collective-permute-start.4) | collective-permute-done | bytes 655392 | tf_op jit(solution)/shard_map/ppermute | solution.py:219
  95.3 5.1 collective-permute-start.7
  102.8 8.6 %collective-permute-done.6 = bf16[4,32,2560]{2,1,0:T(8,128)(2,1)S(1)} collective-permute-done((bf16[4,32,2560]{2,1,0:T(8,128)(2,1)S(1)}, bf16[4,32,2560]{2,1,0:T(8,128)(2,1)S(1)}, u32[]{:S(2)}, u32[]{:S(2)}) %collective-permute-start.6) | collective-permute-done | bytes 655392 | tf_op jit(solution)/shard_map/ppermute | solution.py:219
  114.1 5.1 collective-permute-start.9
  121.5 7.7 %collective-permute-done.8 = bf16[4,32,2560]{2,1,0:T(8,128)(2,1)S(1)} collective-permute-done((bf16[4,32,2560]{2,1,0:T(8,128)(2,1)S(1)}, bf16[4,32,2560]{2,1,0:T(8,128)(2,1)S(1)}, u32[]{:S(2)}, u32[]{:S(2)}) %collective-permute-start.8) | collective-permute-done | bytes 655392 | tf_op jit(solution)/shard_map/ppermute | solution.py:219
  131.9 5.1 collective-permute-start.11
  139.4 6.8 %collective-permute-done.10 = bf16[4,32,2560]{2,1,0:T(8,128)(2,1)S(1)} collective-permute-done((bf16[4,32,2560]{2,1,0:T(8,128)(2,1)S(1)}, bf16[4,32,2560]{2,1,0:T(8,128)(2,1)S(1)}, u32[]{:S(2)}, u32[]{:S(2)}) %collective-permute-start.10) | collective-permute-done | bytes 655392 | tf_op jit(solution)/shard_map/ppermute | solution.py:219
  148.1 5.6 %collective-permute-start.13 = (bf16[4,32,2560]{2,1,0:T(8,128)(2,1)S(1)}, bf16[4,32,2560]{2,1,0:T(8,128)(2,1)}, u32[]{:S(2)}, u32[]{:S(2)}) collective-permute-start(bf16[4,32,2560]{2,1,0:T(8,128)(2,1)S(1)} %collective-permute-done.11), channel_id=1, source_target_pairs={{0,60},{1,61},{2,62},{3,63},{4,0},{5,1},{6,2},{7,3},{8,4},{9,5},{1... | collective-permute-start | bytes 1966088 | tf_op jit(solution)/shard_map/ppermute | solution.py:220
  156.7 5.5 %collective-permute-done.12 = bf16[4,32,2560]{2,1,0:T(8,128)(2,1)} collective-permute-done((bf16[4,32,2560]{2,1,0:T(8,128)(2,1)S(1)}, bf16[4,32,2560]{2,1,0:T(8,128)(2,1)}, u32[]{:S(2)}, u32[]{:S(2)}) %collective-permute-start.12) | collective-permute-done | bytes 655392 | tf_op jit(solution)/shard_map/ppermute | solution.py:219
  164.2 5.3 collective-permute-start.15
  181.3 5.1 collective-permute-start.17
  192.7 1.9 collective-permute-start.18
  196.2 5.4 collective-permute-start.19
  208.2 8.8 %conditional.16 = ((bf16[128,2048]{1,0:T(8,128)(2,1)S(1)}, bf16[128,1024]{1,0:T(8,128)(2,1)S(1)}, bf16[128,256]{1,0:T(8,128)(2,1)S(1)}, bf16[128,256]{1,0:T(8,12...) conditional(s32[]{:T(128)} %convert_element_type.96, ...), branch_computations={%region_3.4_spmd, %region_4.5_spmd} | conditional | bytes 2523212 | solution.py:418
  208.6 8.4 %branch_1_fun.16 = (bf16[128,2048]{1,0:T(8,128)(2,1)S(1)}, bf16[128,1024]{1,0:T(8,128)(2,1)S(1)}, bf16[128,256]{1,0:T(8,128)(2,1)S(1)}, bf16[128,256]{1,0:T(8,12...) custom-call(bf16[128,2048]{1,0:T(8,128)(2,1)S(1)} %get-tuple-element.542.x_ref, ...), custom_call_target="tpu_custom_call" | custom-call | tf_op jit(solution)/shard_map/cond/branch_1_fun/pallas_call | solution.py:196
  217.0 2.1 collective-permute-start.20
  226.8 3.3 conditional.22
  231.9 5.5 %conditional.24 = ((bf16[128,2048]{1,0:T(8,128)(2,1)}, bf16[128,1024]{1,0:T(8,128)(2,1)}, bf16[128,256]{1,0:T(8,128)(2,1)}, bf16[128,128]{1,0:T(8,128)(2,1)})) conditional(s32[]{:T(128)} %convert_element_type.89, bf16[128,2048]{1,0:T(8,128)(2,1)S(1)} %copy-done.2, (bf16[128,2048]{1,0:T(8,128)(2,1)S(1)}, bf16[128,2048]{1,0:T(8,128)(2,1)S(1)}, ...), branch_computations={%region_19.20_spmd, %region_20.21_spmd} | conditional | bytes 1409070 | solution.py:440
  240.8 4.0 conditional.26
  247.2 5.2 conditional.28
  257.7 3.7 conditional.30
  262.8 191.5 %collective-permute-done.33 = bf16[128,2048]{1,0:T(8,128)(2,1)S(1)} collective-permute-done((bf16[128,2048]{1,0:T(8,128)(2,1)}, bf16[128,2048]{1,0:T(8,128)(2,1)S(1)}, u32[]{:S(2)}, u32[]{:S(2)}) %collective-permute-start.33) | collective-permute-done | bytes 524320 | tf_op jit(solution)/shard_map/ppermute | solution.py:442
  454.3 14.6 %conditional.31 = ((bf16[128,1024]{1,0:T(8,128)(2,1)}, bf16[128,256]{1,0:T(8,128)(2,1)}, bf16[128,128]{1,0:T(8,128)(2,1)})) conditional(s32[]{:T(128)} %convert_element_type.96, (bf16[128,1024]{1,0:T(8,128)(2,1)}, bf16[128,256]{1,0:T(8,128)(2,1)}, bf16[128,128]{1,0:T(8,128)(2,1)}) %tuple.136, (pred[]{:T(512)}, bf16[128,2048]{1,0:T(8,128)(2,1)S(1)}, ...), branch_computations={%region_33.34_spmd, %region_34.35_spmd} | conditional | flops 262144 | bytes 3932221 | solution.py:440
  456.4 12.5 %branch_1_fun.31 = (bf16[128,2048]{1,0:T(8,128)(2,1)}, bf16[128,1024]{1,0:T(8,128)(2,1)}, bf16[128,256]{1,0:T(8,128)(2,1)}, bf16[128,128]{1,0:T(8,128)(2,1)}) custom-call(bf16[128,2048]{1,0:T(8,128)(2,1)S(1)} %broadcast_select_fusion.c_ref, bf16[128,2048]{1,0:T(8,128)(2,1)S(1)} %get-tuple-element.729.x_ref, f32[1,2048]{1,0:T(1,128)S(1)} %get-tuple-element.730.gain_ref, ...), custom_call_target="tpu_custom_call" | custom-call | tf_op jit(solution)/shard_map/cond/branch_1_fun/pallas_call | solution.py:196
  470.9 2.8 collective-permute-start.36
  473.7 2.5 collective-permute-start.35
  476.2 4.5 collective-permute-start.34
  482.8 10.0 %collective-permute-start.39 = (bf16[48,512]{1,0:T(8,128)(2,1)S(1)}, bf16[48,512]{1,0:T(8,128)(2,1)S(1)}, u32[]{:S(2)}, u32[]{:S(2)}) collective-permute-start(bf16[48,512]{1,0:T(8,128)(2,1)S(1)} %get-tuple-element.1117), channel_id=1, source_target_pairs={{0,12},{1,13},{2,14},{3,15},{4,0},{5,1},{6,2},{7,3},{8,4},{9,5},{1... | collective-permute-start | bytes 147464 | tf_op jit(solution)/shard_map/ppermute | solution.py:295
  492.8 1.9 collective-permute-start.38
  494.7 2.5 collective-permute-start.37
  497.2 4.0 collective-permute-done.38
  504.5 11.1 %collective-permute-start.41 = (bf16[48,512]{1,0:T(8,128)(2,1)S(1)}, bf16[48,512]{1,0:T(8,128)(2,1)S(1)}, u32[]{:S(2)}, u32[]{:S(2)}) collective-permute-start(bf16[48,512]{1,0:T(8,128)(2,1)S(1)} %fusion.24), channel_id=1, source_target_pairs={{0,32},{1,33},{2,34},{3,35},{4,36},{5,37},{6,38},{7,39},{8,40},{9,... | collective-permute-start | bytes 147464 | tf_op jit(solution)/shard_map/ppermute | solution.py:299
  515.5 2.2 collective-permute-start.40
  519.2 6.3 %collective-permute-done.40 = bf16[48,512]{1,0:T(8,128)(2,1)S(1)} collective-permute-done((bf16[48,512]{1,0:T(8,128)(2,1)S(1)}, bf16[48,512]{1,0:T(8,128)(2,1)S(1)}, u32[]{:S(2)}, u32[]{:S(2)}) %collective-permute-start.40) | collective-permute-done | bytes 49184 | tf_op jit(solution)/shard_map/ppermute | solution.py:299
  525.5 5.1 collective-permute-start.43
  530.6 3.3 collective-permute-start.44
  535.9 2.2 collective-permute-done.44
  538.4 2.7 collective-permute-done.45
  (244 shorter events, 112.9 us)
Async XLA Ops:
  3.1 34.7 %collective-permute-start = (bf16[32,2560]{1,0:T(8,128)(2,1)}, bf16[32,2560]{1,0:T(8,128)(2,1)S(1)}, u32[]{:S(2)}, u32[]{:S(2)}) collective-permute-start(bf16[32,2560]{1,0:T(8,128)(2,1)} %maximum_maximum_fusion.1), channel_id=1, source_target_pairs={{0,1},{1,2},{2,3},{3,0},{4,5},{5,6},{6,7},{7,4},{8,9},{9,10},{10,1... | collective-permute-start | bytes 491528 | tf_op jit(solution)/shard_map/ppermute | solution.py:219
  10.9 29.4 %collective-permute-start.1 = (bf16[32,2560]{1,0:T(8,128)(2,1)}, bf16[32,2560]{1,0:T(8,128)(2,1)}, u32[]{:S(2)}, u32[]{:S(2)}) collective-permute-start(bf16[32,2560]{1,0:T(8,128)(2,1)} %maximum_maximum_fusion.1), channel_id=1, source_target_pairs={{0,3},{1,0},{2,1},{3,2},{4,7},{5,4},{6,5},{7,6},{8,11},{9,8},{10,9... | collective-permute-start | bytes 491528 | tf_op jit(solution)/shard_map/ppermute | solution.py:220
  16.5 160.0 %all-to-all-start = ((bf16[64,4,2048]{2,1,0:T(4,128)(2,1)}), bf16[64,4,2048]{2,1,0:T(4,128)(2,1)S(1)}, u32[]{:S(2)}, u32[]{:S(2)}) async-start(bf16[64,4,2048]{2,1,0:T(4,128)(2,1)} %reshape.177), calls=%async_computation | async-start | bytes 2097152 | tf_op jit(solution)/shard_map/all_to_all | solution.py:320
  37.9 7.7 %collective-permute-start.2 = (bf16[16,2560]{1,0:T(8,128)(2,1)S(1)}, bf16[16,2560]{1,0:T(8,128)(2,1)S(1)}, u32[]{:S(2)}, u32[]{:S(2)}) collective-permute-start(bf16[16,2560]{1,0:T(8,128)(2,1)S(1)} %slice.258), channel_id=1, source_target_pairs={{0,1},{1,2},{2,3},{3,0},{4,5},{5,6},{6,7},{7,4},{8,9},{9,10},{10,1... | collective-permute-start | bytes 245768 | tf_op jit(solution)/shard_map/ppermute | solution.py:224
  41.2 7.9 %collective-permute-start.3 = (bf16[16,2560]{1,0:T(8,128)(2,1)S(1)}, bf16[16,2560]{1,0:T(8,128)(2,1)S(1)}, u32[]{:S(2)}, u32[]{:S(2)}) collective-permute-start(bf16[16,2560]{1,0:T(8,128)(2,1)S(1)} %slice.259), channel_id=1, source_target_pairs={{0,3},{1,0},{2,1},{3,2},{4,7},{5,4},{6,5},{7,6},{8,11},{9,8},{10,9... | collective-permute-start | bytes 245768 | tf_op jit(solution)/shard_map/ppermute | solution.py:225
  49.0 43.6 %collective-permute-start.4 = (bf16[4,32,2560]{2,1,0:T(8,128)(2,1)S(1)}, bf16[4,32,2560]{2,1,0:T(8,128)(2,1)S(1)}, u32[]{:S(2)}, u32[]{:S(2)}) collective-permute-start(bf16[4,32,2560]{2,1,0:T(8,128)(2,1)S(1)} %bitcast_dynamic-update-slice_fusion.4), channel_id=1, source_target_pairs={{0,4},{1,5},{2,6},{3,7},{4,8},{5,9},{6,10},{7,11},{8,12},{9,13},{1... | collective-permute-start | bytes 1966088 | tf_op jit(solution)/shard_map/ppermute | solution.py:219
  52.3 43.0 %collective-permute-start.5 = (bf16[4,32,2560]{2,1,0:T(8,128)(2,1)S(1)}, bf16[4,32,2560]{2,1,0:T(8,128)(2,1)S(1)}, u32[]{:S(2)}, u32[]{:S(2)}) collective-permute-start(bf16[4,32,2560]{2,1,0:T(8,128)(2,1)S(1)} %bitcast_dynamic-update-slice_fusion.4), channel_id=1, source_target_pairs={{0,60},{1,61},{2,62},{3,63},{4,0},{5,1},{6,2},{7,3},{8,4},{9,5},{1... | collective-permute-start | bytes 1966088 | tf_op jit(solution)/shard_map/ppermute | solution.py:220
  92.6 18.8 %collective-permute-start.6 = (bf16[4,32,2560]{2,1,0:T(8,128)(2,1)S(1)}, bf16[4,32,2560]{2,1,0:T(8,128)(2,1)S(1)}, u32[]{:S(2)}, u32[]{:S(2)}) collective-permute-start(bf16[4,32,2560]{2,1,0:T(8,128)(2,1)S(1)} %collective-permute-done.4), channel_id=1, source_target_pairs={{0,4},{1,5},{2,6},{3,7},{4,8},{5,9},{6,10},{7,11},{8,12},{9,13},{1... | collective-permute-start | bytes 1966088 | tf_op jit(solution)/shard_map/ppermute | solution.py:219
  95.3 18.8 %collective-permute-start.7 = (bf16[4,32,2560]{2,1,0:T(8,128)(2,1)S(1)}, bf16[4,32,2560]{2,1,0:T(8,128)(2,1)S(1)}, u32[]{:S(2)}, u32[]{:S(2)}) collective-permute-start(bf16[4,32,2560]{2,1,0:T(8,128)(2,1)S(1)} %collective-permute-done.5), channel_id=1, source_target_pairs={{0,60},{1,61},{2,62},{3,63},{4,0},{5,1},{6,2},{7,3},{8,4},{9,5},{1... | collective-permute-start | bytes 1966088 | tf_op jit(solution)/shard_map/ppermute | solution.py:220
  111.4 17.8 %collective-permute-start.8 = (bf16[4,32,2560]{2,1,0:T(8,128)(2,1)S(1)}, bf16[4,32,2560]{2,1,0:T(8,128)(2,1)S(1)}, u32[]{:S(2)}, u32[]{:S(2)}) collective-permute-start(bf16[4,32,2560]{2,1,0:T(8,128)(2,1)S(1)} %collective-permute-done.6), channel_id=1, source_target_pairs={{0,4},{1,5},{2,6},{3,7},{4,8},{5,9},{6,10},{7,11},{8,12},{9,13},{1... | collective-permute-start | bytes 1966088 | tf_op jit(solution)/shard_map/ppermute | solution.py:219
  114.1 17.9 %collective-permute-start.9 = (bf16[4,32,2560]{2,1,0:T(8,128)(2,1)S(1)}, bf16[4,32,2560]{2,1,0:T(8,128)(2,1)S(1)}, u32[]{:S(2)}, u32[]{:S(2)}) collective-permute-start(bf16[4,32,2560]{2,1,0:T(8,128)(2,1)S(1)} %collective-permute-done.7), channel_id=1, source_target_pairs={{0,60},{1,61},{2,62},{3,63},{4,0},{5,1},{6,2},{7,3},{8,4},{9,5},{1... | collective-permute-start | bytes 1966088 | tf_op jit(solution)/shard_map/ppermute | solution.py:220
  129.2 16.9 %collective-permute-start.10 = (bf16[4,32,2560]{2,1,0:T(8,128)(2,1)S(1)}, bf16[4,32,2560]{2,1,0:T(8,128)(2,1)S(1)}, u32[]{:S(2)}, u32[]{:S(2)}) collective-permute-start(bf16[4,32,2560]{2,1,0:T(8,128)(2,1)S(1)} %collective-permute-done.8), channel_id=1, source_target_pairs={{0,4},{1,5},{2,6},{3,7},{4,8},{5,9},{6,10},{7,11},{8,12},{9,13},{1... | collective-permute-start | bytes 1966088 | tf_op jit(solution)/shard_map/ppermute | solution.py:219
  131.9 16.2 %collective-permute-start.11 = (bf16[4,32,2560]{2,1,0:T(8,128)(2,1)S(1)}, bf16[4,32,2560]{2,1,0:T(8,128)(2,1)S(1)}, u32[]{:S(2)}, u32[]{:S(2)}) collective-permute-start(bf16[4,32,2560]{2,1,0:T(8,128)(2,1)S(1)} %collective-permute-done.9), channel_id=1, source_target_pairs={{0,60},{1,61},{2,62},{3,63},{4,0},{5,1},{6,2},{7,3},{8,4},{9,5},{1... | collective-permute-start | bytes 1966088 | tf_op jit(solution)/shard_map/ppermute | solution.py:220
  146.2 16.1 %collective-permute-start.12 = (bf16[4,32,2560]{2,1,0:T(8,128)(2,1)S(1)}, bf16[4,32,2560]{2,1,0:T(8,128)(2,1)}, u32[]{:S(2)}, u32[]{:S(2)}) collective-permute-start(bf16[4,32,2560]{2,1,0:T(8,128)(2,1)S(1)} %collective-permute-done.10), channel_id=1, source_target_pairs={{0,4},{1,5},{2,6},{3,7},{4,8},{5,9},{6,10},{7,11},{8,12},{9,13},{1... | collective-permute-start | bytes 1966088 | tf_op jit(solution)/shard_map/ppermute | solution.py:219
  148.1 16.1 %collective-permute-start.13 = (bf16[4,32,2560]{2,1,0:T(8,128)(2,1)S(1)}, bf16[4,32,2560]{2,1,0:T(8,128)(2,1)}, u32[]{:S(2)}, u32[]{:S(2)}) collective-permute-start(bf16[4,32,2560]{2,1,0:T(8,128)(2,1)S(1)} %collective-permute-done.11), channel_id=1, source_target_pairs={{0,60},{1,61},{2,62},{3,63},{4,0},{5,1},{6,2},{7,3},{8,4},{9,5},{1... | collective-permute-start | bytes 1966088 | tf_op jit(solution)/shard_map/ppermute | solution.py:220
  162.3 15.4 %collective-permute-start.14 = (bf16[4,32,2560]{2,1,0:T(8,128)(2,1)}, bf16[4,32,2560]{2,1,0:T(8,128)(2,1)}, u32[]{:S(2)}, u32[]{:S(2)}) collective-permute-start(bf16[4,32,2560]{2,1,0:T(8,128)(2,1)} %collective-permute-done.12), channel_id=1, source_target_pairs={{0,4},{1,5},{2,6},{3,7},{4,8},{5,9},{6,10},{7,11},{8,12},{9,13},{1... | collective-permute-start | bytes 1966088 | tf_op jit(solution)/shard_map/ppermute | solution.py:219
  164.2 17.1 %collective-permute-start.15 = (bf16[4,32,2560]{2,1,0:T(8,128)(2,1)}, bf16[4,32,2560]{2,1,0:T(8,128)(2,1)}, u32[]{:S(2)}, u32[]{:S(2)}) collective-permute-start(bf16[4,32,2560]{2,1,0:T(8,128)(2,1)} %collective-permute-done.13), channel_id=1, source_target_pairs={{0,60},{1,61},{2,62},{3,63},{4,0},{5,1},{6,2},{7,3},{8,4},{9,5},{1... | collective-permute-start | bytes 1966088 | tf_op jit(solution)/shard_map/ppermute | solution.py:220
  177.7 15.0 %collective-permute-start.16 = (bf16[4,32,2560]{2,1,0:T(8,128)(2,1)}, bf16[4,32,2560]{2,1,0:T(8,128)(2,1)S(1)}, u32[]{:S(2)}, u32[]{:S(2)}) collective-permute-start(bf16[4,32,2560]{2,1,0:T(8,128)(2,1)} %collective-permute-done.14), channel_id=1, source_target_pairs={{0,4},{1,5},{2,6},{3,7},{4,8},{5,9},{6,10},{7,11},{8,12},{9,13},{1... | collective-permute-start | bytes 1966088 | tf_op jit(solution)/shard_map/ppermute | solution.py:219
  181.3 14.8 %collective-permute-start.17 = (bf16[4,32,2560]{2,1,0:T(8,128)(2,1)}, bf16[4,32,2560]{2,1,0:T(8,128)(2,1)S(1)}, u32[]{:S(2)}, u32[]{:S(2)}) collective-permute-start(bf16[4,32,2560]{2,1,0:T(8,128)(2,1)} %collective-permute-done.15), channel_id=1, source_target_pairs={{0,60},{1,61},{2,62},{3,63},{4,0},{5,1},{6,2},{7,3},{8,4},{9,5},{1... | collective-permute-start | bytes 1966088 | tf_op jit(solution)/shard_map/ppermute | solution.py:220
  192.7 12.0 %collective-permute-start.18 = (bf16[2,32,2560]{2,1,0:T(8,128)(2,1)S(1)}, bf16[2,32,2560]{2,1,0:T(8,128)(2,1)S(1)}, u32[]{:S(2)}, u32[]{:S(2)}) collective-permute-start(bf16[2,32,2560]{2,1,0:T(8,128)(2,1)S(1)} %slice.275), channel_id=1, source_target_pairs={{0,4},{1,5},{2,6},{3,7},{4,8},{5,9},{6,10},{7,11},{8,12},{9,13},{1... | collective-permute-start | bytes 983048 | tf_op jit(solution)/shard_map/ppermute | solution.py:224
  196.2 10.0 %collective-permute-start.19 = (bf16[2,32,2560]{2,1,0:T(8,128)(2,1)S(1)}, bf16[2,32,2560]{2,1,0:T(8,128)(2,1)S(1)}, u32[]{:S(2)}, u32[]{:S(2)}) collective-permute-start(bf16[2,32,2560]{2,1,0:T(8,128)(2,1)S(1)} %slice.277), channel_id=1, source_target_pairs={{0,60},{1,61},{2,62},{3,63},{4,0},{5,1},{6,2},{7,3},{8,4},{9,5},{1... | collective-permute-start | bytes 983048 | tf_op jit(solution)/shard_map/ppermute | solution.py:225
  217.0 2.9 collective-permute-start.20
  220.9 0.7 collective-permute-start.21
  222.5 0.7 collective-permute-start.22
  224.3 0.7 collective-permute-start.23
  225.1 0.7 collective-permute-start.24
  226.0 0.7 collective-permute-start.25
  230.1 0.7 collective-permute-start.26
  237.4 0.7 collective-permute-start.27
  240.1 0.7 collective-permute-start.28
  244.8 0.7 collective-permute-start.29
  246.4 0.7 collective-permute-start.30
  252.4 0.7 collective-permute-start.31
  255.9 0.7 collective-permute-start.32
  261.4 192.9 %collective-permute-start.33 = (bf16[128,2048]{1,0:T(8,128)(2,1)}, bf16[128,2048]{1,0:T(8,128)(2,1)S(1)}, u32[]{:S(2)}, u32[]{:S(2)}) collective-permute-start(bf16[128,2048]{1,0:T(8,128)(2,1)} %get-tuple-element.915), channel_id=1, source_target_pairs={{64,0},{65,1},{66,2},{67,3},{68,4},{69,5},{70,6},{71,7},{72,8},{73... | collective-permute-start | bytes 1572872 | tf_op jit(solution)/shard_map/ppermute | solution.py:442
  468.9 75.0 %copy-start.1 = (bf16[256,2048]{1,0:T(8,128)(2,1)S(1)}, bf16[256,2048]{1,0:T(8,128)(2,1)}, u32[]{:S(2)}) copy-start(bf16[256,2048]{1,0:T(8,128)(2,1)} %param.43) | copy-start | bytes 3145732
  470.9 9.9 %collective-permute-start.36 = (bf16[48,512]{1,0:T(8,128)(2,1)S(1)}, bf16[48,512]{1,0:T(8,128)(2,1)S(1)}, u32[]{:S(2)}, u32[]{:S(2)}) collective-permute-start(bf16[48,512]{1,0:T(8,128)(2,1)S(1)} %get-tuple-element.1156), channel_id=1, source_target_pairs={{0,3},{1,0},{2,1},{3,2},{4,7},{5,4},{6,5},{7,6},{8,11},{9,8},{10,9... | collective-permute-start | bytes 147464 | tf_op jit(solution)/shard_map/ppermute | solution.py:286
  473.7 7.5 %collective-permute-start.35 = (bf16[48,512]{1,0:T(8,128)(2,1)S(1)}, bf16[48,512]{1,0:T(8,128)(2,1)S(1)}, u32[]{:S(2)}, u32[]{:S(2)}) collective-permute-start(bf16[48,512]{1,0:T(8,128)(2,1)S(1)} %get-tuple-element.1157), channel_id=1, source_target_pairs={{0,2},{1,3},{2,0},{3,1},{4,6},{5,7},{6,4},{7,5},{8,10},{9,11},{10,... | collective-permute-start | bytes 147464 | tf_op jit(solution)/shard_map/ppermute | solution.py:286
  476.2 6.6 %collective-permute-start.34 = (bf16[48,512]{1,0:T(8,128)(2,1)S(1)}, bf16[48,512]{1,0:T(8,128)(2,1)S(1)}, u32[]{:S(2)}, u32[]{:S(2)}) collective-permute-start(bf16[48,512]{1,0:T(8,128)(2,1)S(1)} %get-tuple-element.1155), channel_id=1, source_target_pairs={{0,1},{1,2},{2,3},{3,0},{4,5},{5,6},{6,7},{7,4},{8,9},{9,10},{10,1... | collective-permute-start | bytes 147464 | tf_op jit(solution)/shard_map/ppermute | solution.py:286
  482.8 14.4 %collective-permute-start.39 = (bf16[48,512]{1,0:T(8,128)(2,1)S(1)}, bf16[48,512]{1,0:T(8,128)(2,1)S(1)}, u32[]{:S(2)}, u32[]{:S(2)}) collective-permute-start(bf16[48,512]{1,0:T(8,128)(2,1)S(1)} %get-tuple-element.1117), channel_id=1, source_target_pairs={{0,12},{1,13},{2,14},{3,15},{4,0},{5,1},{6,2},{7,3},{8,4},{9,5},{1... | collective-permute-start | bytes 147464 | tf_op jit(solution)/shard_map/ppermute | solution.py:295
  492.8 8.4 %collective-permute-start.38 = (bf16[48,512]{1,0:T(8,128)(2,1)S(1)}, bf16[48,512]{1,0:T(8,128)(2,1)S(1)}, u32[]{:S(2)}, u32[]{:S(2)}) collective-permute-start(bf16[48,512]{1,0:T(8,128)(2,1)S(1)} %get-tuple-element.1117), channel_id=1, source_target_pairs={{0,8},{1,9},{2,10},{3,11},{4,12},{5,13},{6,14},{7,15},{8,0},{9,1},... | collective-permute-start | bytes 147464 | tf_op jit(solution)/shard_map/ppermute | solution.py:295
  494.7 7.8 %collective-permute-start.37 = (bf16[48,512]{1,0:T(8,128)(2,1)S(1)}, bf16[48,512]{1,0:T(8,128)(2,1)S(1)}, u32[]{:S(2)}, u32[]{:S(2)}) collective-permute-start(bf16[48,512]{1,0:T(8,128)(2,1)S(1)} %get-tuple-element.1117), channel_id=1, source_target_pairs={{0,4},{1,5},{2,6},{3,7},{4,8},{5,9},{6,10},{7,11},{8,12},{9,13},{1... | collective-permute-start | bytes 147464 | tf_op jit(solution)/shard_map/ppermute | solution.py:295
  502.5 15.3 %collective-permute-start.42 = (bf16[48,512]{1,0:T(8,128)(2,1)S(1)}, bf16[48,512]{1,0:T(8,128)(2,1)S(1)}, u32[]{:S(2)}, u32[]{:S(2)}) collective-permute-start(bf16[48,512]{1,0:T(8,128)(2,1)S(1)} %fusion.24), channel_id=1, source_target_pairs={{0,48},{1,49},{2,50},{3,51},{4,52},{5,53},{6,54},{7,55},{8,56},{9,... | collective-permute-start | bytes 147464 | tf_op jit(solution)/shard_map/ppermute | solution.py:299
  504.5 14.7 %collective-permute-start.41 = (bf16[48,512]{1,0:T(8,128)(2,1)S(1)}, bf16[48,512]{1,0:T(8,128)(2,1)S(1)}, u32[]{:S(2)}, u32[]{:S(2)}) collective-permute-start(bf16[48,512]{1,0:T(8,128)(2,1)S(1)} %fusion.24), channel_id=1, source_target_pairs={{0,32},{1,33},{2,34},{3,35},{4,36},{5,37},{6,38},{7,39},{8,40},{9,... | collective-permute-start | bytes 147464 | tf_op jit(solution)/shard_map/ppermute | solution.py:299
  515.5 9.9 %collective-permute-start.40 = (bf16[48,512]{1,0:T(8,128)(2,1)S(1)}, bf16[48,512]{1,0:T(8,128)(2,1)S(1)}, u32[]{:S(2)}, u32[]{:S(2)}) collective-permute-start(bf16[48,512]{1,0:T(8,128)(2,1)S(1)} %fusion.24), channel_id=1, source_target_pairs={{0,16},{1,17},{2,18},{3,19},{4,20},{5,21},{6,22},{7,23},{8,24},{9,... | collective-permute-start | bytes 147464 | tf_op jit(solution)/shard_map/ppermute | solution.py:299
  525.5 10.4 %collective-permute-start.43 = (bf16[48,512]{1,0:T(8,128)(2,1)S(1)}, bf16[48,512]{1,0:T(8,128)(2,1)S(1)}, u32[]{:S(2)}, u32[]{:S(2)}) collective-permute-start(bf16[48,512]{1,0:T(8,128)(2,1)S(1)} %get-tuple-element.1115), channel_id=1, source_target_pairs={{0,1},{1,2},{2,3},{3,0},{4,5},{5,6},{6,7},{7,4},{8,9},{9,10},{10,1... | collective-permute-start | bytes 147464 | tf_op jit(solution)/shard_map/ppermute | solution.py:304
  530.6 7.5 %collective-permute-start.44 = (bf16[48,512]{1,0:T(8,128)(2,1)S(1)}, bf16[48,512]{1,0:T(8,128)(2,1)S(1)}, u32[]{:S(2)}, u32[]{:S(2)}) collective-permute-start(bf16[48,512]{1,0:T(8,128)(2,1)S(1)} %get-tuple-element.1115), channel_id=1, source_target_pairs={{0,2},{1,3},{2,0},{3,1},{4,6},{5,7},{6,4},{7,5},{8,10},{9,11},{10,... | collective-permute-start | bytes 147464 | tf_op jit(solution)/shard_map/ppermute | solution.py:304
  533.9 7.2 %collective-permute-start.45 = (bf16[48,512]{1,0:T(8,128)(2,1)S(1)}, bf16[48,512]{1,0:T(8,128)(2,1)S(1)}, u32[]{:S(2)}, u32[]{:S(2)}) collective-permute-start(bf16[48,512]{1,0:T(8,128)(2,1)S(1)} %get-tuple-element.1115), channel_id=1, source_target_pairs={{0,3},{1,0},{2,1},{3,2},{4,7},{5,4},{6,5},{7,6},{8,11},{9,8},{10,9... | collective-permute-start | bytes 147464 | tf_op jit(solution)/shard_map/ppermute | solution.py:304
  (11 other events, 213.7 us)

commit v2 on v1

--- a/solution.py
+++ b/solution.py
@@ -25,7 +25,8 @@
 
 F32 = jnp.float32
 BF16 = jnp.bfloat16
-VMEM_LIMIT = 40 * 1024 * 1024
+VMEM_LIMIT = 20 * 1024 * 1024
+CUTS = (2, 5, 8)
 
 
 def dot(a, b):
@@ -92,8 +93,9 @@
 
 def forward_kernel(
     x_ref, gain_ref, wqkv_ref, wout_ref, down_ref, upq_ref, upv_ref, cos_ref, sin_ref, mask_ref,
-    y_ref, q_ref, k_ref, v_ref, p_ref, low_ref, n_ref,
+    y_ref, kept_x_ref, q_ref, k_ref, v_ref, p_ref, low_ref, n_ref,
 ):
+    kept_x_ref[...] = x_ref[...]
     hidden = x_ref[...].astype(F32)
     energy = jnp.mean(hidden * hidden, axis=-1, keepdims=True)
     n = (hidden * lax.rsqrt(energy + NORM_EPS) * gain_ref[...]).astype(BF16)
@@ -212,64 +214,55 @@
     ]
 
 
-def ring(piece, route, count, place, put, split):
-    put(place, None, piece)
-    ahead = behind = piece
-    for step in range(1, count // 2):
-        ahead = lax.ppermute(ahead, "dp", route(1))
-        behind = lax.ppermute(behind, "dp", route(-1))
-        put((place - step) % count, None, ahead)
-        put((place + step) % count, None, behind)
-    step = count // 2
-    ahead = lax.ppermute(split(ahead)[0], "dp", route(1))
-    behind = lax.ppermute(split(behind)[1], "dp", route(-1))
-    put((place - step) % count, 0, ahead)
-    put((place + step) % count, 1, behind)
-
-
 def gather_weights(shard, replica, replicas):
     rows, columns = shard.shape
     z_count = replicas // X_CHIPS
     z, x = replica // X_CHIPS, replica % X_CHIPS
-    line = [jnp.zeros((X_CHIPS, rows, columns), shard.dtype)]
-
-    def put_line(at, part, data):
-        start = rows // 2 if part == 1 else 0
-        line[0] = lax.dynamic_update_slice(line[0], data[None], (at, start, 0))
-
-    ring(
-        shard,
-        functools.partial(x_route, replicas),
-        X_CHIPS,
-        x,
-        put_line,
-        lambda t: (t[: rows // 2], t[rows // 2 :]),
-    )
+    along_z = functools.partial(z_route, replicas)
+    along_x = functools.partial(x_route, replicas)
     qkv_width = QUERY_WIDTH + 2 * KEY_WIDTH
     half = rows // 2
-    qkv = [jnp.zeros((z_count, X_CHIPS, rows, qkv_width), shard.dtype)]
-    out = [jnp.zeros((z_count, X_CHIPS, half, 2 * QUERY_WIDTH), shard.dtype)]
-
-    def put_plane(at, part, data):
-        start = X_CHIPS // 2 if part == 1 else 0
-        qkv[0] = lax.dynamic_update_slice(qkv[0], data[None, :, :, :qkv_width], (at, start, 0, 0))
-        left = data[None, :, :half, qkv_width:]
-        right = data[None, :, half:, qkv_width:]
-        out[0] = lax.dynamic_update_slice(
-            out[0], jnp.concatenate([left, right], axis=-1), (at, start, 0, 0)
-        )
-
-    ring(
-        line[0],
-        functools.partial(z_route, replicas),
-        z_count,
-        z,
-        put_plane,
-        lambda t: (t[: X_CHIPS // 2], t[X_CHIPS // 2 :]),
-    )
+    qkv = jnp.zeros((z_count, X_CHIPS, rows, qkv_width), shard.dtype)
+    out = jnp.zeros((z_count, X_CHIPS, half, 2 * QUERY_WIDTH), shard.dtype)
+
+    def put(qkv, out, z_at, x_at, data):
+        qkv = lax.dynamic_update_slice(qkv, data[None, None, :, :qkv_width], (z_at, x_at, 0, 0))
+        sides = [data[:half, qkv_width:], data[half:, qkv_width:]]
+        sides = jnp.concatenate(sides, axis=-1)[None, None]
+        return qkv, lax.dynamic_update_slice(out, sides, (z_at, x_at, 0, 0))
+
+    ahead = behind = shard
+    fresh = [(z, shard)]
+    late = None
+    for step in range(1, z_count // 2 + 1):
+        if step < z_count // 2:
+            ahead = lax.ppermute(ahead, "dp", along_z(1))
+            behind = lax.ppermute(behind, "dp", along_z(-1))
+            fresh += [((z - step) % z_count, ahead), ((z + step) % z_count, behind)]
+        else:
+            upper = lax.ppermute(ahead[:half], "dp", along_z(1))
+            lower = lax.ppermute(behind[half:], "dp", along_z(-1))
+            fresh.append(((z + step) % z_count, jnp.concatenate([upper, lower], axis=0)))
+        if step not in CUTS:
+            continue
+        chunk = jnp.stack([data for _, data in fresh])
+        right = lax.ppermute(chunk, "dp", along_x(1))
+        left = lax.ppermute(chunk, "dp", along_x(-1))
+        far_upper = lax.ppermute(right[:, :half], "dp", along_x(1))
+        far_lower = lax.ppermute(left[:, half:], "dp", along_x(-1))
+        for i, (z_at, data) in enumerate(fresh):
+            far = jnp.concatenate([far_upper[i], far_lower[i]], axis=0)
+            qkv, out = put(qkv, out, z_at, x, data)
+            qkv, out = put(qkv, out, z_at, (x - 1) % X_CHIPS, right[i])
+            qkv, out = put(qkv, out, z_at, (x + 1) % X_CHIPS, left[i])
+            qkv, out = put(qkv, out, z_at, (x + 2) % X_CHIPS, far)
+        fresh = []
+        if step == CUTS[1]:
+            late = left
     return (
-        qkv[0].reshape(replicas * rows, qkv_width),
-        out[0].reshape(replicas * half, 2 * QUERY_WIDTH),
+        qkv.reshape(replicas * rows, qkv_width),
+        out.reshape(replicas * half, 2 * QUERY_WIDTH),
+        late,
     )
 
 
@@ -306,7 +299,7 @@
     return whole.transpose(1, 0, 2).reshape(rows, columns)
 
 
-def exchange_tokens(source_tokens, send_counts, replica, replicas, stream_count):
+def exchange_tokens(source_tokens, send_counts, replica, replicas, stream_count, late):
     slot_count = source_tokens.shape[0] // replicas
     features = source_tokens.shape[1]
     sent_counts = lax.dynamic_index_in_dim(send_counts, replica, 0, keepdims=False)
@@ -317,6 +310,7 @@
     own_rows = jnp.arange(source_tokens.shape[0], dtype=jnp.int32)
     choose = (pick_rows[:, None] == own_rows[None, :]).astype(BF16)
     packed = dot(choose, source_tokens).astype(BF16).reshape(replicas, slot_count, features)
+    packed, _ = lax.optimization_barrier((packed, late))
     arrived = lax.all_to_all(packed, "dp", split_axis=0, concat_axis=0, tiled=True)
     incoming = lax.dynamic_index_in_dim(send_counts, replica, 1, keepdims=False)
     end_rows = jnp.cumsum(incoming)
@@ -377,9 +371,9 @@
     shard = jnp.concatenate(
         [query_weight[0], frozen_key_matrix[0], frozen_value_matrix[0], out_rows], axis=1
     )
-    stream, filled = exchange_tokens(source_tokens, send_counts, replica, replicas, tokens)
+    wqkv, wout, late = gather_weights(shard, replica, replicas)
+    stream, filled = exchange_tokens(source_tokens, send_counts, replica, replicas, tokens, late)
     cosine, sine, allowed = layout(doc_segments, filled)
-    wqkv, wout = gather_weights(shard, replica, replicas)
     gain = norm_gain[0].reshape(1, features)
     spare = LANES - 2 * RANK
     down = jnp.concatenate(
@@ -396,6 +390,7 @@
     )
 
     saved_shapes = [
+        ((tokens, features), BF16),
         ((tokens, QUERY_WIDTH), BF16),
         ((tokens, KEY_WIDTH), BF16),
         ((tokens, KEY_WIDTH), BF16),
@@ -417,10 +412,9 @@
 
         y, saved = lax.cond(section == turn, run, lambda x, saved: (x, saved), x, saved)
         if turn + 1 < sections:
-            came = lax.ppermute(y, "section", [(turn, turn + 1)])
-            x = jnp.where(section == turn + 1, came, x)
-
-    q, k, v, shares, low, normed = saved
+            x = lax.ppermute(y, "section", [(turn, turn + 1)])
+
+    x, q, k, v, shares, low, normed = saved
     c = out_cotangent
     kept = (
         jnp.zeros((tokens, QUERY_WIDTH), BF16),
@@ -439,8 +433,7 @@
 
         back, kept = lax.cond(section == turn, run_back, lambda c, kept: (c, kept), c, kept)
         if turn > 0:
-            came = lax.ppermute(back, "section", [(turn, turn - 1)])
-            c = jnp.where(section == turn - 1, came, c)
+            c = lax.ppermute(back, "section", [(turn, turn - 1)])
 
     (grads,) = call(
         grads_kernel, [((3 * RANK, features), F32)], normed, low, kept[0], kept[1], kept[2]

time: 553 us -> 622 us (1.12)
  other arithmetic: 22.7 us -> 61.9 us
  waiting for transfers between devices: 277 us -> 244 us
  starting transfers between devices: 149 us -> 180 us
  local copies, waits for them, and re-layouts: 53.1 us -> 75.7 us
  loops' own time: 16.2 us -> 24.1 us
    dynamic_update_slice x18 -> x81, other arithmetic: 12.3 us -> 51.4 us  [the longest x64 40.4 us: put(): return (qkv, lax.dynamic_update_slice(out, sides, (z_at, x_at, 0, 0)))]
    ppermute x34 -> x42, starting transfers between devices: 84.4 us -> 120 us  [the longest x7 39.5 us: gather_weights(): behind = lax.ppermute(behind, 'dp', along_z(-1))]
    ppermute x34 -> x42, waiting for transfers between devices: 257 us -> 225 us  [the longest x7 206 us: local(): c = lax.ppermute(back, 'section', [(turn, turn - 1)])]
    dynamic_update_slice x21 -> x47, local copies, waits for them, and re-layouts: 18.1 us -> 30.4 us  [put(): lax.dynamic_update_slice(qkv, data[None, None, :, :qkv_width], (z_at, x_a...]
    cond x15 -> x1, local copies, waits for them, and re-layouts: 10.9 us -> 1.04 us
    unnamed x25 -> x115, local copies, waits for them, and re-layouts: 2.48 us -> 11.1 us
    slice x4 -> x76, local copies, waits for them, and re-layouts: 0.95 us -> 9.2 us  [the longest x68 5.93 us: put(): sides = [data[:half, qkv_width:], data[half:, qkv_width:]]]
    another operation x8, loops' own time: 13.2 us -> 20.1 us  [local(): lax.cond(section == turn, run_back, lambda c, kept: (c, kept), c, kept)]
  transfers between devices with their start and end apart: 47 -> 55, of which waited for: 20 -> 18; matrix products, arithmetic and copies ran while one was open for 9% -> 21% of each run, Pallas kernels for 0% -> 0%
where the time goes in v2:
time: 622 us; the launch traced here: 613 us
  waiting for transfers between devices  244 us (39%)
  starting transfers between devices  180 us (29%)
  local copies, waits for them, and re-layouts  75.7 us (12%)
  other arithmetic  61.9 us (10%)
  loops' own time  24.1 us (4%)
  Pallas kernels  23.2 us (4%)
    ppermute x7, waiting for transfers between devices, local(): c = lax.ppermute(back, 'section', [(turn, turn - 1)])  206 us
    dynamic_update_slice x64, other arithmetic, put(): return (qkv, lax.dynamic_update_slice(out, sides, (z_at, x_at, 0, 0)))  40.4 us
    ppermute x7, starting transfers between devices, gather_weights(): behind = lax.ppermute(behind, 'dp', along_z(-1))  39.5 us
    dynamic_update_slice x47, local copies, waits for them, and re-layouts, put(): lax.dynamic_update_slice(qkv, data[None, None, :, :qkv_width], (z_at, x_a...  30.4 us
    ppermute x6, starting transfers between devices, sum_over_replicas(): total = total + lax.ppermute(sent, 'dp', route).astype(F32)  29.4 us
    pallas_call x3, Pallas kernels, call(): pl.pallas_call(kernel, out_shape=[jax.ShapeDtypeStruct(shape, dtype) for...  23.2 us
    another operation x8, loops' own time, local(): lax.cond(section == turn, run_back, lambda c, kept: (c, kept), c, kept)  20.1 us
    ppermute x7, starting transfers between devices, gather_weights(): ahead = lax.ppermute(ahead, 'dp', along_z(1))  15.3 us
  transfers between devices with their start and end apart: 55, of which 18 were waited for; matrix products, arithmetic and copies ran while one was open for 21% of the time, Pallas kernels for 0%

profile of v2, /device:TPU:6, one launch (start us, length us, event | category | flops | bytes accessed | tf_op | source)
XLA Modules:
  0.0 613.0 jit_solution(1802296624683283681)
XLA Ops:
  5.0 3.8 collective-permute-start
  8.8 9.5 %collective-permute-start.3 = (bf16[32,2560]{1,0:T(8,128)(2,1)}, bf16[32,2560]{1,0:T(8,128)(2,1)S(1)}, u32[]{:S(2)}, u32[]{:S(2)}) collective-permute-start(bf16[32,2560]{1,0:T(8,128)(2,1)} %maximum_maximum_fusion.1), channel_id=1, source_target_pairs={{0,60},{1,61},{2,62},{3,63},{4,0},{5,1},{6,2},{7,3},{8,4},{9,5},{1... | collective-permute-start | bytes 491528 | tf_op jit(solution)/shard_map/ppermute | solution.py:240
  25.3 3.4 broadcast_in_dim.465
  29.4 2.6 broadcast_in_dim.530
  44.9 5.1 collective-permute-start.4
  53.6 2.4 collective-permute-start.11
  55.9 3.5 collective-permute-start.12
  61.3 5.6 collective-permute-start.5
  70.9 5.1 collective-permute-start.7
  80.6 5.1 collective-permute-start.9
  89.3 2.7 collective-permute-start.10
  92.0 4.3 collective-permute-start.15
  99.5 5.7 collective-permute-done.18
  105.2 3.9 collective-permute-start.19
  115.7 5.1 collective-permute-start.21
  124.4 5.1 collective-permute-start.13
  135.3 3.7 collective-permute-done.22
  139.0 2.7 collective-permute-start.23
  141.8 3.6 collective-permute-done.23
  148.0 3.9 collective-permute-start.25
  175.1 12.1 %all-to-all-start = ((bf16[64,4,2048]{2,1,0:T(4,128)(2,1)}), bf16[64,4,2048]{2,1,0:T(4,128)(2,1)S(1)}, u32[]{:S(2)}, u32[]{:S(2)}) async-start(bf16[64,4,2048]{2,1,0:T(4,128)(2,1)} %reshape.177), calls=%async_computation | async-start | bytes 2097152 | tf_op jit(solution)/shard_map/all_to_all | solution.py:314
  187.2 2.8 collective-permute-start.17
  191.1 4.3 collective-permute-start.16
  203.7 5.4 collective-permute-start.26
  266.4 10.5 %conditional.16 = ((bf16[128,2048]{1,0:T(8,128)(2,1)}, bf16[128,2048]{1,0:T(8,128)(2,1)S(1)}, bf16[128,1024]{1,0:T(8,128)(2,1)S(1)}, bf16[128,256]{1,0:T(8,128)(...) conditional(s32[]{:T(128)} %convert_element_type.96, ...), branch_computations={%region_3.4_spmd, %region_4.5_spmd} | conditional | bytes 1998934 | solution.py:413
  267.6 9.2 %branch_1_fun.16 = (bf16[128,2048]{1,0:T(8,128)(2,1)}, bf16[128,2048]{1,0:T(8,128)(2,1)S(1)}, bf16[128,1024]{1,0:T(8,128)(2,1)S(1)}, bf16[128,256]{1,0:T(8,128)(...) custom-call(bf16[128,2048]{1,0:T(8,128)(2,1)S(1)} %copy.421.x_ref, ...), custom_call_target="tpu_custom_call" | custom-call | tf_op jit(solution)/shard_map/cond/branch_1_fun/pallas_call | solution.py:198
  286.0 3.8 conditional.21
  291.9 5.1 conditional.24
  299.9 4.4 conditional.26
  307.2 4.6 conditional.28
  314.7 6.1 conditional.30
  322.1 205.8 %collective-permute-done.41 = bf16[128,2048]{1,0:T(8,128)(2,1)S(1)} collective-permute-done((bf16[128,2048]{1,0:T(8,128)(2,1)}, bf16[128,2048]{1,0:T(8,128)(2,1)S(1)}, u32[]{:S(2)}, u32[]{:S(2)}) %collective-permute-start.41) | collective-permute-done | bytes 524320 | tf_op jit(solution)/shard_map/ppermute | solution.py:436
  527.9 12.6 %conditional.31 = ((bf16[128,1024]{1,0:T(8,128)(2,1)S(1)}, bf16[128,256]{1,0:T(8,128)(2,1)S(1)}, bf16[128,128]{1,0:T(8,128)(2,1)S(1)})) conditional(s32[]{:T(128)} %convert_element_type.96, (bf16[128,1024]{1,0:T(8,128)(2,1)S(1)}, bf16[128,256]{1,0:T(8,128)(2,1)S(1)}, bf16[128,128]{1,0:T(8,128)(2,1)S(1)}) %tuple.138, ...), branch_computations={%region_33.34_spmd, %region_34.35_spmd} | conditional | bytes 262176 | solution.py:434
  528.1 12.4 %branch_1_fun.31 = (bf16[128,2048]{1,0:T(8,128)(2,1)}, bf16[128,1024]{1,0:T(8,128)(2,1)S(1)}, bf16[128,256]{1,0:T(8,128)(2,1)S(1)}, bf16[128,128]{1,0:T(8,128)(2,1)S(1)}) custom-call(bf16[128,2048]{1,0:T(8,128)(2,1)S(1)} %get-tuple-element.735.c_ref, bf16[128,2048]{1,0:T(8,128)(2,1)S(1)} %get-tuple-element.736.x_ref, ...), custom_call_target="tpu_custom_call" | custom-call | tf_op jit(solution)/shard_map/cond/branch_1_fun/pallas_call | solution.py:198
  544.3 4.6 collective-permute-start.43
  548.9 2.5 collective-permute-start.42
  551.8 3.1 collective-permute-done.42
  554.9 5.7 collective-permute-start.47
  562.6 2.5 collective-permute-start.45
  565.0 2.5 collective-permute-done.46
  567.5 3.2 collective-permute-done.45
  570.7 5.9 collective-permute-start.50
  576.6 7.9 %collective-permute-start.49 = (bf16[48,512]{1,0:T(8,128)(2,1)S(1)}, bf16[48,512]{1,0:T(8,128)(2,1)S(1)}, u32[]{:S(2)}, u32[]{:S(2)}) collective-permute-start(bf16[48,512]{1,0:T(8,128)(2,1)S(1)} %fusion.151), channel_id=1, source_target_pairs={{0,32},{1,33},{2,34},{3,35},{4,36},{5,37},{6,38},{7,39},{8,40},{9,... | collective-permute-start | bytes 147464 | tf_op jit(solution)/shard_map/ppermute | solution.py:292
  584.5 5.5 collective-permute-start.48
  591.4 3.5 collective-permute-done.48
  594.9 4.2 collective-permute-start.51
  599.2 3.7 collective-permute-start.52
  606.9 3.1 collective-permute-done.53
  (482 shorter events, 189.4 us)
Async XLA Ops:
  5.0 37.9 %collective-permute-start = (bf16[32,2560]{1,0:T(8,128)(2,1)}, bf16[32,2560]{1,0:T(8,128)(2,1)S(1)}, u32[]{:S(2)}, u32[]{:S(2)}) collective-permute-start(bf16[32,2560]{1,0:T(8,128)(2,1)} %maximum_maximum_fusion.1), channel_id=1, source_target_pairs={{0,4},{1,5},{2,6},{3,7},{4,8},{5,9},{6,10},{7,11},{8,12},{9,13},{1... | collective-permute-start | bytes 491528 | tf_op jit(solution)/shard_map/ppermute | solution.py:239
  8.8 36.0 %collective-permute-start.3 = (bf16[32,2560]{1,0:T(8,128)(2,1)}, bf16[32,2560]{1,0:T(8,128)(2,1)S(1)}, u32[]{:S(2)}, u32[]{:S(2)}) collective-permute-start(bf16[32,2560]{1,0:T(8,128)(2,1)} %maximum_maximum_fusion.1), channel_id=1, source_target_pairs={{0,60},{1,61},{2,62},{3,63},{4,0},{5,1},{6,2},{7,3},{8,4},{9,5},{1... | collective-permute-start | bytes 491528 | tf_op jit(solution)/shard_map/ppermute | solution.py:240
  42.9 8.8 %collective-permute-start.1 = (bf16[32,2560]{1,0:T(8,128)(2,1)S(1)}, bf16[32,2560]{1,0:T(8,128)(2,1)S(1)}, u32[]{:S(2)}, u32[]{:S(2)}) collective-permute-start(bf16[32,2560]{1,0:T(8,128)(2,1)S(1)} %collective-permute-done), channel_id=1, source_target_pairs={{0,4},{1,5},{2,6},{3,7},{4,8},{5,9},{6,10},{7,11},{8,12},{9,13},{1... | collective-permute-start | bytes 491528 | tf_op jit(solution)/shard_map/ppermute | solution.py:239
  44.9 8.0 %collective-permute-start.4 = (bf16[32,2560]{1,0:T(8,128)(2,1)S(1)}, bf16[32,2560]{1,0:T(8,128)(2,1)S(1)}, u32[]{:S(2)}, u32[]{:S(2)}) collective-permute-start(bf16[32,2560]{1,0:T(8,128)(2,1)S(1)} %collective-permute-done.3), channel_id=1, source_target_pairs={{0,60},{1,61},{2,62},{3,63},{4,0},{5,1},{6,2},{7,3},{8,4},{9,5},{1... | collective-permute-start | bytes 491528 | tf_op jit(solution)/shard_map/ppermute | solution.py:240
  53.6 67.3 %collective-permute-start.11 = (bf16[5,32,2560]{2,1,0:T(8,128)(2,1)}, bf16[5,32,2560]{2,1,0:T(8,128)(2,1)S(1)}, u32[]{:S(2)}, u32[]{:S(2)}) collective-permute-start(bf16[5,32,2560]{2,1,0:T(8,128)(2,1)} %bitcast_dynamic-update-slice_fusion.5), channel_id=1, source_target_pairs={{0,1},{1,2},{2,3},{3,0},{4,5},{5,6},{6,7},{7,4},{8,9},{9,10},{10,1... | collective-permute-start | bytes 2457608 | tf_op jit(solution)/shard_map/ppermute | solution.py:249
  55.9 59.7 %collective-permute-start.12 = (bf16[5,32,2560]{2,1,0:T(8,128)(2,1)}, bf16[5,32,2560]{2,1,0:T(8,128)(2,1)S(1)}, u32[]{:S(2)}, u32[]{:S(2)}) collective-permute-start(bf16[5,32,2560]{2,1,0:T(8,128)(2,1)} %bitcast_dynamic-update-slice_fusion.5), channel_id=1, source_target_pairs={{0,3},{1,0},{2,1},{3,2},{4,7},{5,4},{6,5},{7,6},{8,11},{9,8},{10,9... | collective-permute-start | bytes 2457608 | tf_op jit(solution)/shard_map/ppermute | solution.py:250
  59.4 8.9 %collective-permute-start.2 = (bf16[32,2560]{1,0:T(8,128)(2,1)S(1)}, bf16[32,2560]{1,0:T(8,128)(2,1)S(1)}, u32[]{:S(2)}, u32[]{:S(2)}) collective-permute-start(bf16[32,2560]{1,0:T(8,128)(2,1)S(1)} %collective-permute-done.1), channel_id=1, source_target_pairs={{0,4},{1,5},{2,6},{3,7},{4,8},{5,9},{6,10},{7,11},{8,12},{9,13},{1... | collective-permute-start | bytes 491528 | tf_op jit(solution)/shard_map/ppermute | solution.py:239
  61.3 9.6 %collective-permute-start.5 = (bf16[32,2560]{1,0:T(8,128)(2,1)S(1)}, bf16[32,2560]{1,0:T(8,128)(2,1)S(1)}, u32[]{:S(2)}, u32[]{:S(2)}) collective-permute-start(bf16[32,2560]{1,0:T(8,128)(2,1)S(1)} %collective-permute-done.4), channel_id=1, source_target_pairs={{0,60},{1,61},{2,62},{3,63},{4,0},{5,1},{6,2},{7,3},{8,4},{9,5},{1... | collective-permute-start | bytes 491528 | tf_op jit(solution)/shard_map/ppermute | solution.py:240
  69.0 8.4 %collective-permute-start.6 = (bf16[32,2560]{1,0:T(8,128)(2,1)S(1)}, bf16[32,2560]{1,0:T(8,128)(2,1)S(1)}, u32[]{:S(2)}, u32[]{:S(2)}) collective-permute-start(bf16[32,2560]{1,0:T(8,128)(2,1)S(1)} %collective-permute-done.2), channel_id=1, source_target_pairs={{0,4},{1,5},{2,6},{3,7},{4,8},{5,9},{6,10},{7,11},{8,12},{9,13},{1... | collective-permute-start | bytes 491528 | tf_op jit(solution)/shard_map/ppermute | solution.py:239
  70.9 9.7 %collective-permute-start.7 = (bf16[32,2560]{1,0:T(8,128)(2,1)S(1)}, bf16[32,2560]{1,0:T(8,128)(2,1)S(1)}, u32[]{:S(2)}, u32[]{:S(2)}) collective-permute-start(bf16[32,2560]{1,0:T(8,128)(2,1)S(1)} %collective-permute-done.5), channel_id=1, source_target_pairs={{0,60},{1,61},{2,62},{3,63},{4,0},{5,1},{6,2},{7,3},{8,4},{9,5},{1... | collective-permute-start | bytes 491528 | tf_op jit(solution)/shard_map/ppermute | solution.py:240
  77.4 9.7 %collective-permute-start.8 = (bf16[32,2560]{1,0:T(8,128)(2,1)S(1)}, bf16[32,2560]{1,0:T(8,128)(2,1)S(1)}, u32[]{:S(2)}, u32[]{:S(2)}) collective-permute-start(bf16[32,2560]{1,0:T(8,128)(2,1)S(1)} %collective-permute-done.6), channel_id=1, source_target_pairs={{0,4},{1,5},{2,6},{3,7},{4,8},{5,9},{6,10},{7,11},{8,12},{9,13},{1... | collective-permute-start | bytes 491528 | tf_op jit(solution)/shard_map/ppermute | solution.py:239
  80.6 8.0 %collective-permute-start.9 = (bf16[32,2560]{1,0:T(8,128)(2,1)S(1)}, bf16[32,2560]{1,0:T(8,128)(2,1)S(1)}, u32[]{:S(2)}, u32[]{:S(2)}) collective-permute-start(bf16[32,2560]{1,0:T(8,128)(2,1)S(1)} %collective-permute-done.7), channel_id=1, source_target_pairs={{0,60},{1,61},{2,62},{3,63},{4,0},{5,1},{6,2},{7,3},{8,4},{9,5},{1... | collective-permute-start | bytes 491528 | tf_op jit(solution)/shard_map/ppermute | solution.py:240
  89.3 85.8 %collective-permute-start.10 = (bf16[6,32,2560]{2,1,0:T(8,128)(2,1)}, bf16[6,32,2560]{2,1,0:T(8,128)(2,1)S(1)}, u32[]{:S(2)}, u32[]{:S(2)}) collective-permute-start(bf16[6,32,2560]{2,1,0:T(8,128)(2,1)} %bitcast_dynamic-update-slice_fusion.10), channel_id=1, source_target_pairs={{0,3},{1,0},{2,1},{3,2},{4,7},{5,4},{6,5},{7,6},{8,11},{9,8},{10,9... | collective-permute-start | bytes 2949128 | tf_op jit(solution)/shard_map/ppermute | solution.py:250
  92.0 98.0 %collective-permute-start.15 = (bf16[6,32,2560]{2,1,0:T(8,128)(2,1)}, bf16[6,32,2560]{2,1,0:T(8,128)(2,1)}, u32[]{:S(2)}, u32[]{:S(2)}) collective-permute-start(bf16[6,32,2560]{2,1,0:T(8,128)(2,1)} %bitcast_dynamic-update-slice_fusion.10), channel_id=1, source_target_pairs={{0,1},{1,2},{2,3},{3,0},{4,5},{5,6},{6,7},{7,4},{8,9},{9,10},{10,1... | collective-permute-start | bytes 2949128 | tf_op jit(solution)/shard_map/ppermute | solution.py:249
  96.3 8.9 %collective-permute-start.18 = (bf16[32,2560]{1,0:T(8,128)(2,1)S(1)}, bf16[32,2560]{1,0:T(8,128)(2,1)S(1)}, u32[]{:S(2)}, u32[]{:S(2)}) collective-permute-start(bf16[32,2560]{1,0:T(8,128)(2,1)S(1)} %collective-permute-done.8), channel_id=1, source_target_pairs={{0,4},{1,5},{2,6},{3,7},{4,8},{5,9},{6,10},{7,11},{8,12},{9,13},{1... | collective-permute-start | bytes 491528 | tf_op jit(solution)/shard_map/ppermute | solution.py:239
  105.2 7.2 %collective-permute-start.19 = (bf16[32,2560]{1,0:T(8,128)(2,1)S(1)}, bf16[32,2560]{1,0:T(8,128)(2,1)S(1)}, u32[]{:S(2)}, u32[]{:S(2)}) collective-permute-start(bf16[32,2560]{1,0:T(8,128)(2,1)S(1)} %collective-permute-done.9), channel_id=1, source_target_pairs={{0,60},{1,61},{2,62},{3,63},{4,0},{5,1},{6,2},{7,3},{8,4},{9,5},{1... | collective-permute-start | bytes 491528 | tf_op jit(solution)/shard_map/ppermute | solution.py:240
  112.4 11.9 %collective-permute-start.20 = (bf16[32,2560]{1,0:T(8,128)(2,1)S(1)}, bf16[32,2560]{1,0:T(8,128)(2,1)S(1)}, u32[]{:S(2)}, u32[]{:S(2)}) collective-permute-start(bf16[32,2560]{1,0:T(8,128)(2,1)S(1)} %collective-permute-done.18), channel_id=1, source_target_pairs={{0,4},{1,5},{2,6},{3,7},{4,8},{5,9},{6,10},{7,11},{8,12},{9,13},{1... | collective-permute-start | bytes 491528 | tf_op jit(solution)/shard_map/ppermute | solution.py:239
  115.7 15.8 %collective-permute-start.21 = (bf16[32,2560]{1,0:T(8,128)(2,1)S(1)}, bf16[32,2560]{1,0:T(8,128)(2,1)S(1)}, u32[]{:S(2)}, u32[]{:S(2)}) collective-permute-start(bf16[32,2560]{1,0:T(8,128)(2,1)S(1)} %collective-permute-done.19), channel_id=1, source_target_pairs={{0,60},{1,61},{2,62},{3,63},{4,0},{5,1},{6,2},{7,3},{8,4},{9,5},{1... | collective-permute-start | bytes 491528 | tf_op jit(solution)/shard_map/ppermute | solution.py:240
  120.9 27.2 %collective-permute-start.14 = (bf16[5,16,2560]{2,1,0:T(8,128)(2,1)S(1)}, bf16[5,16,2560]{2,1,0:T(8,128)(2,1)S(1)}, u32[]{:S(2)}, u32[]{:S(2)}) collective-permute-start(bf16[5,16,2560]{2,1,0:T(8,128)(2,1)S(1)} %slice.1090), channel_id=1, source_target_pairs={{0,3},{1,0},{2,1},{3,2},{4,7},{5,4},{6,5},{7,6},{8,11},{9,8},{10,9... | collective-permute-start | bytes 1228808 | tf_op jit(solution)/shard_map/ppermute | solution.py:252
  124.4 27.6 %collective-permute-start.13 = (bf16[5,16,2560]{2,1,0:T(8,128)(2,1)S(1)}, bf16[5,16,2560]{2,1,0:T(8,128)(2,1)S(1)}, u32[]{:S(2)}, u32[]{:S(2)}) collective-permute-start(bf16[5,16,2560]{2,1,0:T(8,128)(2,1)S(1)} %slice.1088), channel_id=1, source_target_pairs={{0,1},{1,2},{2,3},{3,0},{4,5},{5,6},{6,7},{7,4},{8,9},{9,10},{10,1... | collective-permute-start | bytes 1228808 | tf_op jit(solution)/shard_map/ppermute | solution.py:251
  131.5 7.5 %collective-permute-start.22 = (bf16[16,2560]{1,0:T(8,128)(2,1)S(1)}, bf16[16,2560]{1,0:T(8,128)(2,1)S(1)}, u32[]{:S(2)}, u32[]{:S(2)}) collective-permute-start(bf16[16,2560]{1,0:T(8,128)(2,1)S(1)} %slice.1165), channel_id=1, source_target_pairs={{0,4},{1,5},{2,6},{3,7},{4,8},{5,9},{6,10},{7,11},{8,12},{9,13},{1... | collective-permute-start | bytes 245768 | tf_op jit(solution)/shard_map/ppermute | solution.py:243
  139.0 6.3 %collective-permute-start.23 = (bf16[16,2560]{1,0:T(8,128)(2,1)S(1)}, bf16[16,2560]{1,0:T(8,128)(2,1)S(1)}, u32[]{:S(2)}, u32[]{:S(2)}) collective-permute-start(bf16[16,2560]{1,0:T(8,128)(2,1)S(1)} %slice.1166), channel_id=1, source_target_pairs={{0,60},{1,61},{2,62},{3,63},{4,0},{5,1},{6,2},{7,3},{8,4},{9,5},{1... | collective-permute-start | bytes 245768 | tf_op jit(solution)/shard_map/ppermute | solution.py:244
  146.1 56.6 %collective-permute-start.24 = (bf16[5,32,2560]{2,1,0:T(8,128)(2,1)}, bf16[5,32,2560]{2,1,0:T(8,128)(2,1)}, u32[]{:S(2)}, u32[]{:S(2)}) collective-permute-start(bf16[5,32,2560]{2,1,0:T(8,128)(2,1)} %bitcast_dynamic-update-slice_fusion), channel_id=1, source_target_pairs={{0,1},{1,2},{2,3},{3,0},{4,5},{5,6},{6,7},{7,4},{8,9},{9,10},{10,1... | collective-permute-start | bytes 2457608 | tf_op jit(solution)/shard_map/ppermute | solution.py:249
  148.0 51.5 %collective-permute-start.25 = (bf16[5,32,2560]{2,1,0:T(8,128)(2,1)}, bf16[5,32,2560]{2,1,0:T(8,128)(2,1)}, u32[]{:S(2)}, u32[]{:S(2)}) collective-permute-start(bf16[5,32,2560]{2,1,0:T(8,128)(2,1)} %bitcast_dynamic-update-slice_fusion), channel_id=1, source_target_pairs={{0,3},{1,0},{2,1},{3,2},{4,7},{5,4},{6,5},{7,6},{8,11},{9,8},{10,9... | collective-permute-start | bytes 2457608 | tf_op jit(solution)/shard_map/ppermute | solution.py:250
  175.1 89.9 %all-to-all-start = ((bf16[64,4,2048]{2,1,0:T(4,128)(2,1)}), bf16[64,4,2048]{2,1,0:T(4,128)(2,1)S(1)}, u32[]{:S(2)}, u32[]{:S(2)}) async-start(bf16[64,4,2048]{2,1,0:T(4,128)(2,1)} %reshape.177), calls=%async_computation | async-start | bytes 2097152 | tf_op jit(solution)/shard_map/all_to_all | solution.py:314
  187.2 24.7 %collective-permute-start.17 = (bf16[6,16,2560]{2,1,0:T(8,128)(2,1)S(1)}, bf16[6,16,2560]{2,1,0:T(8,128)(2,1)S(1)}, u32[]{:S(2)}, u32[]{:S(2)}) collective-permute-start(bf16[6,16,2560]{2,1,0:T(8,128)(2,1)S(1)} %slice.1127), channel_id=1, source_target_pairs={{0,3},{1,0},{2,1},{3,2},{4,7},{5,4},{6,5},{7,6},{8,11},{9,8},{10,9... | collective-permute-start | bytes 1474568 | tf_op jit(solution)/shard_map/ppermute | solution.py:252
  191.1 21.0 %collective-permute-start.16 = (bf16[6,16,2560]{2,1,0:T(8,128)(2,1)S(1)}, bf16[6,16,2560]{2,1,0:T(8,128)(2,1)S(1)}, u32[]{:S(2)}, u32[]{:S(2)}) collective-permute-start(bf16[6,16,2560]{2,1,0:T(8,128)(2,1)S(1)} %slice.1125), channel_id=1, source_target_pairs={{0,1},{1,2},{2,3},{3,0},{4,5},{5,6},{6,7},{7,4},{8,9},{9,10},{10,1... | collective-permute-start | bytes 1474568 | tf_op jit(solution)/shard_map/ppermute | solution.py:251
  200.6 42.4 %collective-permute-start.27 = (bf16[5,16,2560]{2,1,0:T(8,128)(2,1)S(1)}, bf16[5,16,2560]{2,1,0:T(8,128)(2,1)S(1)}, u32[]{:S(2)}, u32[]{:S(2)}) collective-permute-start(bf16[5,16,2560]{2,1,0:T(8,128)(2,1)S(1)} %slice.1173), channel_id=1, source_target_pairs={{0,3},{1,0},{2,1},{3,2},{4,7},{5,4},{6,5},{7,6},{8,11},{9,8},{10,9... | collective-permute-start | bytes 1228808 | tf_op jit(solution)/shard_map/ppermute | solution.py:252
  203.7 39.3 %collective-permute-start.26 = (bf16[5,16,2560]{2,1,0:T(8,128)(2,1)S(1)}, bf16[5,16,2560]{2,1,0:T(8,128)(2,1)S(1)}, u32[]{:S(2)}, u32[]{:S(2)}) collective-permute-start(bf16[5,16,2560]{2,1,0:T(8,128)(2,1)S(1)} %slice.1171), channel_id=1, source_target_pairs={{0,1},{1,2},{2,3},{3,0},{4,5},{5,6},{6,7},{7,4},{8,9},{9,10},{10,1... | collective-permute-start | bytes 1228808 | tf_op jit(solution)/shard_map/ppermute | solution.py:251
  276.8 3.1 collective-permute-start.28
  281.6 1.5 collective-permute-start.30
  289.8 1.5 collective-permute-start.33
  297.0 1.5 collective-permute-start.35
  304.3 1.5 collective-permute-start.37
  311.8 1.5 collective-permute-start.39
  320.8 207.1 %collective-permute-start.41 = (bf16[128,2048]{1,0:T(8,128)(2,1)}, bf16[128,2048]{1,0:T(8,128)(2,1)S(1)}, u32[]{:S(2)}, u32[]{:S(2)}) collective-permute-start(bf16[128,2048]{1,0:T(8,128)(2,1)} %get-tuple-element.940), channel_id=1, source_target_pairs={{64,0},{65,1},{66,2},{67,3},{68,4},{69,5},{70,6},{71,7},{72,8},{73... | collective-permute-start | bytes 1572872 | tf_op jit(solution)/shard_map/ppermute | solution.py:436
  542.4 9.1 %collective-permute-start.44 = (bf16[48,512]{1,0:T(8,128)(2,1)S(1)}, bf16[48,512]{1,0:T(8,128)(2,1)S(1)}, u32[]{:S(2)}, u32[]{:S(2)}) collective-permute-start(bf16[48,512]{1,0:T(8,128)(2,1)S(1)} %get-tuple-element.1209), channel_id=1, source_target_pairs={{0,3},{1,0},{2,1},{3,2},{4,7},{5,4},{6,5},{7,6},{8,11},{9,8},{10,9... | collective-permute-start | bytes 147464 | tf_op jit(solution)/shard_map/ppermute | solution.py:279
  544.3 7.5 %collective-permute-start.43 = (bf16[48,512]{1,0:T(8,128)(2,1)S(1)}, bf16[48,512]{1,0:T(8,128)(2,1)S(1)}, u32[]{:S(2)}, u32[]{:S(2)}) collective-permute-start(bf16[48,512]{1,0:T(8,128)(2,1)S(1)} %get-tuple-element.1210), channel_id=1, source_target_pairs={{0,2},{1,3},{2,0},{3,1},{4,6},{5,7},{6,4},{7,5},{8,10},{9,11},{10,... | collective-permute-start | bytes 147464 | tf_op jit(solution)/shard_map/ppermute | solution.py:279
  548.9 6.0 collective-permute-start.42
  554.9 10.1 %collective-permute-start.47 = (bf16[48,512]{1,0:T(8,128)(2,1)S(1)}, bf16[48,512]{1,0:T(8,128)(2,1)S(1)}, u32[]{:S(2)}, u32[]{:S(2)}) collective-permute-start(bf16[48,512]{1,0:T(8,128)(2,1)S(1)} %get-tuple-element.1140), channel_id=1, source_target_pairs={{0,12},{1,13},{2,14},{3,15},{4,0},{5,1},{6,2},{7,3},{8,4},{9,5},{1... | collective-permute-start | bytes 147464 | tf_op jit(solution)/shard_map/ppermute | solution.py:288
  560.6 6.9 %collective-permute-start.46 = (bf16[48,512]{1,0:T(8,128)(2,1)S(1)}, bf16[48,512]{1,0:T(8,128)(2,1)S(1)}, u32[]{:S(2)}, u32[]{:S(2)}) collective-permute-start(bf16[48,512]{1,0:T(8,128)(2,1)S(1)} %get-tuple-element.1140), channel_id=1, source_target_pairs={{0,8},{1,9},{2,10},{3,11},{4,12},{5,13},{6,14},{7,15},{8,0},{9,1},... | collective-permute-start | bytes 147464 | tf_op jit(solution)/shard_map/ppermute | solution.py:288
  562.6 8.1 %collective-permute-start.45 = (bf16[48,512]{1,0:T(8,128)(2,1)S(1)}, bf16[48,512]{1,0:T(8,128)(2,1)S(1)}, u32[]{:S(2)}, u32[]{:S(2)}) collective-permute-start(bf16[48,512]{1,0:T(8,128)(2,1)S(1)} %get-tuple-element.1140), channel_id=1, source_target_pairs={{0,4},{1,5},{2,6},{3,7},{4,8},{5,9},{6,10},{7,11},{8,12},{9,13},{1... | collective-permute-start | bytes 147464 | tf_op jit(solution)/shard_map/ppermute | solution.py:288
  570.7 19.4 %collective-permute-start.50 = (bf16[48,512]{1,0:T(8,128)(2,1)S(1)}, bf16[48,512]{1,0:T(8,128)(2,1)S(1)}, u32[]{:S(2)}, u32[]{:S(2)}) collective-permute-start(bf16[48,512]{1,0:T(8,128)(2,1)S(1)} %fusion.151), channel_id=1, source_target_pairs={{0,48},{1,49},{2,50},{3,51},{4,52},{5,53},{6,54},{7,55},{8,56},{9,... | collective-permute-start | bytes 147464 | tf_op jit(solution)/shard_map/ppermute | solution.py:292
  576.6 14.8 %collective-permute-start.49 = (bf16[48,512]{1,0:T(8,128)(2,1)S(1)}, bf16[48,512]{1,0:T(8,128)(2,1)S(1)}, u32[]{:S(2)}, u32[]{:S(2)}) collective-permute-start(bf16[48,512]{1,0:T(8,128)(2,1)S(1)} %fusion.151), channel_id=1, source_target_pairs={{0,32},{1,33},{2,34},{3,35},{4,36},{5,37},{6,38},{7,39},{8,40},{9,... | collective-permute-start | bytes 147464 | tf_op jit(solution)/shard_map/ppermute | solution.py:292
  584.5 10.3 %collective-permute-start.48 = (bf16[48,512]{1,0:T(8,128)(2,1)S(1)}, bf16[48,512]{1,0:T(8,128)(2,1)S(1)}, u32[]{:S(2)}, u32[]{:S(2)}) collective-permute-start(bf16[48,512]{1,0:T(8,128)(2,1)S(1)} %fusion.151), channel_id=1, source_target_pairs={{0,16},{1,17},{2,18},{3,19},{4,20},{5,21},{6,22},{7,23},{8,24},{9,... | collective-permute-start | bytes 147464 | tf_op jit(solution)/shard_map/ppermute | solution.py:292
  594.9 9.9 %collective-permute-start.51 = (bf16[48,512]{1,0:T(8,128)(2,1)S(1)}, bf16[48,512]{1,0:T(8,128)(2,1)S(1)}, u32[]{:S(2)}, u32[]{:S(2)}) collective-permute-start(bf16[48,512]{1,0:T(8,128)(2,1)S(1)} %get-tuple-element.1138), channel_id=1, source_target_pairs={{0,1},{1,2},{2,3},{3,0},{4,5},{5,6},{6,7},{7,4},{8,9},{9,10},{10,1... | collective-permute-start | bytes 147464 | tf_op jit(solution)/shard_map/ppermute | solution.py:297
  599.2 7.5 %collective-permute-start.52 = (bf16[48,512]{1,0:T(8,128)(2,1)S(1)}, bf16[48,512]{1,0:T(8,128)(2,1)S(1)}, u32[]{:S(2)}, u32[]{:S(2)}) collective-permute-start(bf16[48,512]{1,0:T(8,128)(2,1)S(1)} %get-tuple-element.1138), channel_id=1, source_target_pairs={{0,2},{1,3},{2,0},{3,1},{4,6},{5,7},{6,4},{7,5},{8,10},{9,11},{10,... | collective-permute-start | bytes 147464 | tf_op jit(solution)/shard_map/ppermute | solution.py:297
  602.8 7.2 %collective-permute-start.53 = (bf16[48,512]{1,0:T(8,128)(2,1)S(1)}, bf16[48,512]{1,0:T(8,128)(2,1)S(1)}, u32[]{:S(2)}, u32[]{:S(2)}) collective-permute-start(bf16[48,512]{1,0:T(8,128)(2,1)S(1)} %get-tuple-element.1138), channel_id=1, source_target_pairs={{0,3},{1,0},{2,1},{3,2},{4,7},{5,4},{6,5},{7,6},{8,11},{9,8},{10,9... | collective-permute-start | bytes 147464 | tf_op jit(solution)/shard_map/ppermute | solution.py:297
  (58 other events, 1281.6 us)

commit v3 on v2

--- a/solution.py
+++ b/solution.py
@@ -25,7 +25,7 @@
 
 F32 = jnp.float32
 BF16 = jnp.bfloat16
-VMEM_LIMIT = 20 * 1024 * 1024
+VMEM_LIMIT = 32 * 1024 * 1024
 CUTS = (2, 5, 8)
 
 
@@ -91,11 +91,29 @@
     return total
 
 
+def load(copies):
+    for copy in copies:
+        copy.start()
+
+
 def forward_kernel(
-    x_ref, gain_ref, wqkv_ref, wout_ref, down_ref, upq_ref, upv_ref, cos_ref, sin_ref, mask_ref,
-    y_ref, kept_x_ref, q_ref, k_ref, v_ref, p_ref, low_ref, n_ref,
+    last,
+    x_hbm, gain_ref, wqkv_hbm, wout_hbm, down_ref, upq_ref, upv_ref, cos_ref, sin_ref, mask_ref,
+    y_ref, x_ref, q_ref, k_ref, v_ref, p_ref, low_ref, n_ref,
+    wqkv, wout, sems,
 ):
-    kept_x_ref[...] = x_ref[...]
+    width = GROUP * HEAD_SIZE
+    head_at = [pl.ds(h * width, width) for h in range(KEY_VALUE_HEADS)]
+    key_at = pl.ds(QUERY_WIDTH, 2 * KEY_WIDTH)
+    get_x = pltpu.make_async_copy(x_hbm, x_ref, sems.at[0])
+    get_kv = pltpu.make_async_copy(wqkv_hbm.at[:, key_at], wqkv.at[:, key_at], sems.at[1])
+    get_q = [
+        pltpu.make_async_copy(wqkv_hbm.at[:, at], wqkv.at[:, at], sems.at[2 + h])
+        for h, at in enumerate(head_at)
+    ]
+    get_out = pltpu.make_async_copy(wout_hbm, wout, sems.at[2 + KEY_VALUE_HEADS])
+    load([get_x, get_kv] + get_q + ([] if last else [get_out]))
+    get_x.wait()
     hidden = x_ref[...].astype(F32)
     energy = jnp.mean(hidden * hidden, axis=-1, keepdims=True)
     n = (hidden * lax.rsqrt(energy + NORM_EPS) * gain_ref[...]).astype(BF16)
@@ -103,19 +121,20 @@
     cosine, sine = cos_ref[...], sin_ref[...]
     low = dot(n, down_ref[...]).astype(BF16)
     low_ref[...] = low
-    k = rope(dot(n, wqkv_ref[:, QUERY_WIDTH : QUERY_WIDTH + KEY_WIDTH]), cosine, sine).astype(BF16)
+    get_kv.wait()
+    kv = dot(n, wqkv[:, key_at])
+    k = rope(kv[:, :KEY_WIDTH], cosine, sine).astype(BF16)
     k_ref[...] = k
-    v = dot(n, wqkv_ref[:, QUERY_WIDTH + KEY_WIDTH :]) + ADAPTER_SCALE * dot(low, upv_ref[...])
+    v = kv[:, KEY_WIDTH:] + ADAPTER_SCALE * dot(low, upv_ref[...])
     v = v.astype(BF16)
     v_ref[...] = v
     k_turns, v_turns = turns_of(k), turns_of(v)
     allowed = mask_ref[...] > 0.0
     tokens = hidden.shape[0]
-    width = GROUP * HEAD_SIZE
     blended = []
-    for h in range(KEY_VALUE_HEADS):
-        at = slice(h * width, (h + 1) * width)
-        q = dot(n, wqkv_ref[:, at]) + ADAPTER_SCALE * dot(low, upq_ref[:, at])
+    for h, at in enumerate(head_at):
+        get_q[h].wait()
+        q = dot(n, wqkv[:, at]) + ADAPTER_SCALE * dot(low, upq_ref[:, at])
         q = rope(q, cosine, sine).astype(BF16)
         q_ref[:, at] = q
         scores = dot_nt(q, expand(k_turns, h)) * SCORE_SCALE
@@ -125,27 +144,55 @@
             shares.append((weights / jnp.sum(weights, axis=-1, keepdims=True)).astype(BF16))
         shares = jnp.concatenate(shares, axis=1)
         p_ref[:, h * GROUP * tokens : (h + 1) * GROUP * tokens] = shares
-        blended.append(dot(shares, expand(v_turns, h)).astype(BF16))
-    blended = jnp.concatenate(blended, axis=1)
-    y_ref[...] = (hidden + dot(blended, wout_ref[...])).astype(BF16)
+        if not last:
+            blended.append(dot(shares, expand(v_turns, h)).astype(BF16))
+    if last:
+        y_ref[...] = jnp.zeros_like(y_ref)
+        return
+    get_out.wait()
+    y_ref[...] = (hidden + dot(jnp.concatenate(blended, axis=1), wout[...])).astype(BF16)
 
 
 def backward_kernel(
-    c_ref, x_ref, gain_ref, wqkv_ref, wout_ref, down_ref, upq_ref, upv_ref, cos_ref, sin_ref,
+    first,
+    c_hbm, x_ref, gain_ref, wqkv_hbm, wout_hbm, down_ref, upq_ref, upv_ref, cos_ref, sin_ref,
     q_ref, k_ref, v_ref, p_ref,
     out_ref, dq_ref, dv_ref, dlow_ref,
+    c_ref, wqkv, wout, sems,
 ):
+    width = GROUP * HEAD_SIZE
+    head_at = [pl.ds(h * width, width) for h in range(KEY_VALUE_HEADS)]
+    key_at = pl.ds(QUERY_WIDTH, 2 * KEY_WIDTH)
+    get_c = pltpu.make_async_copy(c_hbm, c_ref, sems.at[0])
+    get_out = [
+        pltpu.make_async_copy(wout_hbm.at[at, :], wout.at[at, :], sems.at[1 + h])
+        for h, at in enumerate(head_at)
+    ]
+    get_q = [
+        pltpu.make_async_copy(
+            wqkv_hbm.at[:, at], wqkv.at[:, at], sems.at[1 + KEY_VALUE_HEADS + h]
+        )
+        for h, at in enumerate(head_at)
+    ]
+    get_kv = pltpu.make_async_copy(
+        wqkv_hbm.at[:, key_at], wqkv.at[:, key_at], sems.at[1 + 2 * KEY_VALUE_HEADS]
+    )
+    load([get_c])
+    for h in range(KEY_VALUE_HEADS):
+        load([get_out[h]] + ([] if first else [get_q[h]]))
+    if not first:
+        load([get_kv])
+    k_turns, v_turns = turns_of(k_ref[...]), turns_of(v_ref[...])
+    cosine, sine = cos_ref[...], sin_ref[...]
+    get_c.wait()
     c = c_ref[...]
     tokens = c.shape[0]
-    width = GROUP * HEAD_SIZE
-    cosine, sine = cos_ref[...], sin_ref[...]
-    k_turns, v_turns = turns_of(k_ref[...]), turns_of(v_ref[...])
     dn = None
     dlow = None
     dk_products, dv_products = [], []
-    for h in range(KEY_VALUE_HEADS):
-        at = slice(h * width, (h + 1) * width)
-        dblended = dot_nt(c, wout_ref[at, :]).astype(BF16)
+    for h, at in enumerate(head_at):
+        get_out[h].wait()
+        dblended = dot_nt(c, wout[at, :]).astype(BF16)
         shares = p_ref[:, h * GROUP * tokens : (h + 1) * GROUP * tokens]
         dshares = dot_nt(dblended, expand(v_turns, h))
         dscores = []
@@ -163,17 +210,22 @@
         dq_ref[:, at] = dq
         part = dot_nt(dq, upq_ref[:, at])
         dlow = part if dlow is None else dlow + part
-        part = dot_nt(dq, wqkv_ref[:, at])
-        dn = part if dn is None else dn + part
         dv_products.append(dot_tn(shares, dblended))
-        dk_products.append(dot_tn(dscores, q_ref[:, at]))
-    dk = rope(fold(dk_products), cosine, -sine).astype(BF16)
+        if not first:
+            dk_products.append(dot_tn(dscores, q_ref[:, at]))
+            get_q[h].wait()
+            part = dot_nt(dq, wqkv[:, at])
+            dn = part if dn is None else dn + part
     dv = fold(dv_products).astype(BF16)
     dv_ref[...] = dv
     dlow = (ADAPTER_SCALE * (dlow + dot_nt(dv, upv_ref[...]))).astype(BF16)
     dlow_ref[...] = dlow
-    dn = dn + dot_nt(dk, wqkv_ref[:, QUERY_WIDTH : QUERY_WIDTH + KEY_WIDTH])
-    dn = dn + dot_nt(dv, wqkv_ref[:, QUERY_WIDTH + KEY_WIDTH :])
+    if first:
+        out_ref[...] = jnp.zeros_like(out_ref)
+        return
+    dk = rope(fold(dk_products), cosine, -sine).astype(BF16)
+    get_kv.wait()
+    dn = dn + dot_nt(jnp.concatenate([dk, dv], axis=1), wqkv[:, key_at])
     dn = dn + dot_nt(dlow, down_ref[...])
     hidden = x_ref[...].astype(F32)
     energy = jnp.mean(hidden * hidden, axis=-1, keepdims=True)
@@ -185,21 +237,82 @@
 
 
 def grads_kernel(n_ref, low_ref, dq_ref, dv_ref, dlow_ref, g_ref):
-    g_ref[...] = jnp.zeros_like(g_ref)
-    g_ref[0 : 2 * RANK, :] = dot_tn(dlow_ref[...], n_ref[...])[: 2 * RANK]
+    part = g_ref.shape[2]
+    down = dot_tn(dlow_ref[...], n_ref[...])[: 2 * RANK].astype(BF16)
     low = low_ref[...]
-    up_q = ADAPTER_SCALE * dot_tn(low, dq_ref[...])
-    up_v = ADAPTER_SCALE * dot_tn(low, dv_ref[...])
-    g_ref[2 * RANK : 3 * RANK, 0:QUERY_WIDTH] = up_q[:RANK]
-    g_ref[2 * RANK : 3 * RANK, QUERY_WIDTH : QUERY_WIDTH + KEY_WIDTH] = up_v[RANK : 2 * RANK]
-
-
-def call(kernel, outs, *args):
+    up_q = ADAPTER_SCALE * dot_tn(low, dq_ref[...])[:RANK]
+    up_v = ADAPTER_SCALE * dot_tn(low, dv_ref[...])[RANK : 2 * RANK]
+    spare = jnp.zeros((RANK, g_ref.shape[0] * part - QUERY_WIDTH - KEY_WIDTH), F32)
+    up = jnp.concatenate([up_q, up_v, spare], axis=1).astype(BF16)
+    for i in range(g_ref.shape[0]):
+        at = slice(i * part, (i + 1) * part)
+        g_ref[i, 0 : 2 * RANK, :] = down[:, at]
+        g_ref[i, 2 * RANK : 3 * RANK, :] = up[:, at]
+
+
+def place_kernel(offsets, place_ref, *refs):
+    own, right, left, far_upper, far_lower = refs[:5]
+    qkv, out, sems = refs[-3:]
+    z_count, x_count, rows, qkv_width = qkv.shape
+    half, width = rows // 2, out.shape[3] // 2
+    z, x = place_ref[0], place_ref[1]
+    ends = []
+    for i, offset in enumerate(offsets):
+        z_at = lax.rem(z + (offset + z_count), z_count)
+        for source, turn in ((own, 0), (right, x_count - 1), (left, 1)):
+            x_at = lax.rem(x + turn, x_count)
+            ends += [
+                (source.at[i, :, pl.ds(0, qkv_width)], qkv.at[z_at, x_at]),
+                (
+                    source.at[i, pl.ds(0, half), pl.ds(qkv_width, width)],
+                    out.at[z_at, x_at, :, pl.ds(0, width)],
+                ),
+                (
+                    source.at[i, pl.ds(half, half), pl.ds(qkv_width, width)],
+                    out.at[z_at, x_at, :, pl.ds(width, width)],
+                ),
+            ]
+        x_at = lax.rem(x + 2, x_count)
+        for source, side in ((far_upper, 0), (far_lower, 1)):
+            ends += [
+                (
+                    source.at[i, :, pl.ds(0, qkv_width)],
+                    qkv.at[z_at, x_at, pl.ds(side * half, half)],
+                ),
+                (
+                    source.at[i, :, pl.ds(qkv_width, width)],
+                    out.at[z_at, x_at, :, pl.ds(side * width, width)],
+                ),
+            ]
+    copies = [pltpu.make_async_copy(a, b, sems.at[j]) for j, (a, b) in enumerate(ends)]
+    load(copies)
+    for copy in copies:
+        copy.wait()
+
+
+def place(offsets, at, pieces, kept, shapes):
+    anywhere = pl.BlockSpec(memory_space=pl.ANY)
+    first_kept = 1 + len(pieces)
+    return pl.pallas_call(
+        functools.partial(place_kernel, offsets),
+        out_shape=[jax.ShapeDtypeStruct(shape, BF16) for shape in shapes],
+        in_specs=[pl.BlockSpec(memory_space=pltpu.SMEM)] + [anywhere] * (len(pieces) + len(kept)),
+        out_specs=[anywhere] * len(shapes),
+        scratch_shapes=[pltpu.SemaphoreType.DMA((13 * len(offsets),))],
+        input_output_aliases={first_kept + i: i for i in range(len(kept))},
+    )(at, *pieces, *kept)
+
+
+def call(kernel, outs, args, from_hbm=(), scratch=()):
     return pl.pallas_call(
         kernel,
         out_shape=[jax.ShapeDtypeStruct(shape, dtype) for shape, dtype in outs],
-        in_specs=[pl.BlockSpec(memory_space=pltpu.VMEM)] * len(args),
+        in_specs=[
+            pl.BlockSpec(memory_space=pl.ANY if i in from_hbm else pltpu.VMEM)
+            for i in range(len(args))
+        ],
         out_specs=[pl.BlockSpec(memory_space=pltpu.VMEM)] * len(outs),
+        scratch_shapes=list(scratch),
         compiler_params=pltpu.CompilerParams(vmem_limit_bytes=VMEM_LIMIT),
     )(*args)
 
@@ -222,27 +335,24 @@
     along_x = functools.partial(x_route, replicas)
     qkv_width = QUERY_WIDTH + 2 * KEY_WIDTH
     half = rows // 2
-    qkv = jnp.zeros((z_count, X_CHIPS, rows, qkv_width), shard.dtype)
-    out = jnp.zeros((z_count, X_CHIPS, half, 2 * QUERY_WIDTH), shard.dtype)
-
-    def put(qkv, out, z_at, x_at, data):
-        qkv = lax.dynamic_update_slice(qkv, data[None, None, :, :qkv_width], (z_at, x_at, 0, 0))
-        sides = [data[:half, qkv_width:], data[half:, qkv_width:]]
-        sides = jnp.concatenate(sides, axis=-1)[None, None]
-        return qkv, lax.dynamic_update_slice(out, sides, (z_at, x_at, 0, 0))
-
+    shapes = [
+        (z_count, X_CHIPS, rows, qkv_width),
+        (z_count, X_CHIPS, half, 2 * (columns - qkv_width)),
+    ]
+    at = jnp.stack([z, x]).astype(jnp.int32)
+    placed = ()
     ahead = behind = shard
-    fresh = [(z, shard)]
+    fresh = [(0, shard)]
     late = None
     for step in range(1, z_count // 2 + 1):
         if step < z_count // 2:
             ahead = lax.ppermute(ahead, "dp", along_z(1))
             behind = lax.ppermute(behind, "dp", along_z(-1))
-            fresh += [((z - step) % z_count, ahead), ((z + step) % z_count, behind)]
+            fresh += [(-step, ahead), (step, behind)]
         else:
             upper = lax.ppermute(ahead[:half], "dp", along_z(1))
             lower = lax.ppermute(behind[half:], "dp", along_z(-1))
-            fresh.append(((z + step) % z_count, jnp.concatenate([upper, lower], axis=0)))
+            fresh.append((step, jnp.concatenate([upper, lower], axis=0)))
         if step not in CUTS:
             continue
         chunk = jnp.stack([data for _, data in fresh])
@@ -250,53 +360,48 @@
         left = lax.ppermute(chunk, "dp", along_x(-1))
         far_upper = lax.ppermute(right[:, :half], "dp", along_x(1))
         far_lower = lax.ppermute(left[:, half:], "dp", along_x(-1))
-        for i, (z_at, data) in enumerate(fresh):
-            far = jnp.concatenate([far_upper[i], far_lower[i]], axis=0)
-            qkv, out = put(qkv, out, z_at, x, data)
-            qkv, out = put(qkv, out, z_at, (x - 1) % X_CHIPS, right[i])
-            qkv, out = put(qkv, out, z_at, (x + 1) % X_CHIPS, left[i])
-            qkv, out = put(qkv, out, z_at, (x + 2) % X_CHIPS, far)
+        pieces = (chunk, right, left, far_upper, far_lower)
+        placed = place([offset for offset, _ in fresh], at, pieces, placed, shapes)
         fresh = []
         if step == CUTS[1]:
             late = left
     return (
-        qkv.reshape(replicas * rows, qkv_width),
-        out.reshape(replicas * half, 2 * QUERY_WIDTH),
+        placed[0].reshape(replicas * rows, qkv_width),
+        placed[1].reshape(replicas * half, 2 * (columns - qkv_width)),
         late,
     )
 
 
-def sum_over_replicas(grads, replica, replicas):
-    rows, columns = grads.shape
-    z_count = replicas // X_CHIPS
+def sum_over_replicas(parts, replica, replicas):
+    count, rows, columns = parts.shape
     x = replica % X_CHIPS
-    part_width = columns // X_CHIPS
-    parts = grads.reshape(rows, X_CHIPS, part_width).transpose(1, 0, 2)
-    sent = parts.astype(BF16)
-    total = lax.dynamic_index_in_dim(parts, x, 0, keepdims=False)
-    for distance in range(1, X_CHIPS):
-        piece = lax.dynamic_index_in_dim(sent, (x + distance) % X_CHIPS, 0, keepdims=False)
-        total = total + lax.ppermute(piece, "dp", x_route(replicas, distance)).astype(F32)
-    low_count = 4
-    sent = total.astype(BF16)
-    for distance in range(1, low_count):
-        route = []
-        for i in range(replicas):
-            zi, xi = i // X_CHIPS, i % X_CHIPS
-            to = zi // low_count * low_count + (zi % low_count + distance) % low_count
-            route.append((i, to * X_CHIPS + xi))
-        total = total + lax.ppermute(sent, "dp", route).astype(F32)
-    sent = total.astype(BF16)
-    for distance in range(1, z_count // low_count):
-        route = z_route(replicas, distance * low_count)
-        total = total + lax.ppermute(sent, "dp", route).astype(F32)
-    sent = total.astype(BF16)
-    whole = jnp.zeros((X_CHIPS, rows, part_width), F32)
-    whole = lax.dynamic_update_slice(whole, total[None], (x, 0, 0))
-    for distance in range(1, X_CHIPS):
-        piece = lax.ppermute(sent, "dp", x_route(replicas, distance)).astype(F32)
-        whole = lax.dynamic_update_slice(whole, piece[None], ((x - distance) % X_CHIPS, 0, 0))
-    return whole.transpose(1, 0, 2).reshape(rows, columns)
+    low_bit, high_bit = x % 2, x // 2
+
+    def swap(t, mask):
+        return lax.ppermute(t, "dp", [(i, i ^ mask) for i in range(replicas)])
+
+    def add(t, other):
+        return (t.astype(F32) + other.astype(F32)).astype(BF16)
+
+    def pick(t, axis, at):
+        return lax.dynamic_index_in_dim(t, at, axis, keepdims=False)
+
+    def join(own, other, bit, axis):
+        return jnp.where(
+            bit == 0, jnp.stack([own, other], axis=axis), jnp.stack([other, own], axis=axis)
+        )
+
+    total = parts.reshape(2, 2, rows, columns)
+    total = add(pick(total, 1, low_bit), swap(pick(total, 1, 1 - low_bit), 1))
+    total = add(pick(total, 0, high_bit), swap(pick(total, 0, 1 - high_bit), 2))
+    mask = X_CHIPS
+    while mask < replicas:
+        total = add(total, swap(total, mask))
+        mask *= 2
+    total = join(total, swap(total, 2), high_bit, 0)
+    total = join(total, swap(total, 1), low_bit, 1)
+    whole = total.reshape(count, rows, columns).astype(F32)
+    return whole.transpose(1, 0, 2).reshape(rows, count * columns)
 
 
 def exchange_tokens(source_tokens, send_counts, replica, replicas, stream_count, late):
@@ -398,15 +503,18 @@
         ((tokens, LANES), BF16),
         ((tokens, features), BF16),
     ]
+    weight_space = [pltpu.VMEM(wqkv.shape, BF16), pltpu.VMEM(wout.shape, BF16)]
     x = stream
     saved = tuple(jnp.zeros(shape, dtype) for shape, dtype in saved_shapes)
     for turn in range(sections):
 
         def run(x, saved):
             made = call(
-                forward_kernel,
+                functools.partial(forward_kernel, turn + 1 == sections),
                 [((tokens, features), BF16)] + saved_shapes,
-                x, gain, wqkv, wout, down, up_q, up_v, cosine, sine, allowed,
+                (x, gain, wqkv, wout, down, up_q, up_v, cosine, sine, allowed),
+                (0, 2, 3),
+                weight_space + [pltpu.SemaphoreType.DMA((3 + KEY_VALUE_HEADS,))],
             )
             return made[0], tuple(made[1:])
 
@@ -425,9 +533,13 @@
 
         def run_back(c, kept):
             made = call(
-                backward_kernel,
+                functools.partial(backward_kernel, turn == 0),
                 [((tokens, features), BF16)] + [(t.shape, t.dtype) for t in kept],
-                c, x, gain, wqkv, wout, down, up_q, up_v, cosine, sine, q, k, v, shares,
+                (c, x, gain, wqkv, wout, down, up_q, up_v, cosine, sine, q, k, v, shares),
+                (0, 3, 4),
+                [pltpu.VMEM((tokens, features), BF16)]
+                + weight_space
+                + [pltpu.SemaphoreType.DMA((2 + 2 * KEY_VALUE_HEADS,))],
             )
             return made[0], tuple(made[1:])
 
@@ -436,7 +548,9 @@
             c = lax.ppermute(back, "section", [(turn, turn - 1)])
 
     (grads,) = call(
-        grads_kernel, [((3 * RANK, features), F32)], normed, low, kept[0], kept[1], kept[2]
+        grads_kernel,
+        [((X_CHIPS, 3 * RANK, features // X_CHIPS), BF16)],
+        (normed, low, kept[0], kept[1], kept[2]),
     )
     grads = sum_over_replicas(grads, replica, replicas)
     down_grads = grads[: 2 * RANK].reshape(2, RANK, features).transpose(0, 2, 1)

time: 622 us -> 888 us (1.43)
  Pallas kernels: 23.2 us -> 343 us
  waiting for transfers between devices: 244 us -> 298 us
  other arithmetic: 61.9 us -> 10.5 us
  local copies, waits for them, and re-layouts: 75.7 us -> 40.3 us
  starting transfers between devices: 180 us -> 164 us
    pallas_call x0 -> x3, Pallas kernels: none -> 325 us  [place(): pl.pallas_call(functools.partial(place_kernel, offsets), out_shape=[jax.S...]
    dynamic_update_slice x83 -> x0, other arithmetic: 51.4 us -> none  [the longest x64 40.4 us: put(): return (qkv, lax.dynamic_update_slice(out, sides, (z_at, x_at, 0, 0)))]
    dynamic_update_slice x50 -> x0, local copies, waits for them, and re-layouts: 31.6 us -> none  [the longest x47 30.4 us: put(): lax.dynamic_update_slice(qkv, data[None, None, :, :qkv_width], (z_at, x_a...]
    ppermute x12 -> x8, waiting for transfers between devices: 18.7 us -> 43.4 us  [swap(): return lax.ppermute(t, 'dp', [(i, i ^ mask) for i in range(replicas)])]
    ppermute x12 -> x8, starting transfers between devices: 48.2 us -> 23.8 us  [swap(): return lax.ppermute(t, 'dp', [(i, i ^ mask) for i in range(replicas)])]
    ppermute x1, waiting for transfers between devices: 3.68 us -> 23.2 us  [gather_weights(): upper = lax.ppermute(ahead[:half], 'dp', along_z(1))]
    ppermute x7, waiting for transfers between devices: 206 us -> 219 us  [local(): c = lax.ppermute(back, 'section', [(turn, turn - 1)])]
  transfers between devices with their start and end apart: 55 -> 51, of which waited for: 18 -> 18; matrix products, arithmetic and copies ran while one was open for 21% -> 4% of each run, Pallas kernels for 0% -> 37%
where the time goes in v3:
time: 888 us; the launch traced here: 879 us
  Pallas kernels  343 us (39%)
  waiting for transfers between devices  298 us (34%)
  starting transfers between devices  164 us (18%)
  local copies, waits for them, and re-layouts  40.3 us (5%)
  loops' own time  19.1 us (2%)
  other arithmetic  10.5 us (1%)
    pallas_call x3, Pallas kernels, place(): pl.pallas_call(functools.partial(place_kernel, offsets), out_shape=[jax.S...  325 us
    ppermute x7, waiting for transfers between devices, local(): c = lax.ppermute(back, 'section', [(turn, turn - 1)])  219 us
    ppermute x8, waiting for transfers between devices, swap(): return lax.ppermute(t, 'dp', [(i, i ^ mask) for i in range(replicas)])  43.4 us
    ppermute x7, starting transfers between devices, gather_weights(): behind = lax.ppermute(behind, 'dp', along_z(-1))  41.2 us
    ppermute x8, starting transfers between devices, swap(): return lax.ppermute(t, 'dp', [(i, i ^ mask) for i in range(replicas)])  23.8 us
    ppermute x1, waiting for transfers between devices, gather_weights(): upper = lax.ppermute(ahead[:half], 'dp', along_z(1))  23.2 us
    another operation x8, loops' own time, local(): lax.cond(section == turn, run_back, lambda c, kept: (c, kept), c, kept)  18.9 us
    pallas_call x3, Pallas kernels, call(): pl.pallas_call(kernel, out_shape=[jax.ShapeDtypeStruct(shape, dtype) for...  18.5 us
  transfers between devices with their start and end apart: 51, of which 18 were waited for; matrix products, arithmetic and copies ran while one was open for 4% of the time, Pallas kernels for 37%

profile of v3, /device:TPU:6, one launch (start us, length us, event | category | flops | bytes accessed | tf_op | source)
XLA Modules:
  0.0 879.2 jit_solution(10060418308345870453)
XLA Ops:
  4.3 3.8 collective-permute-start
  8.1 9.5 %collective-permute-start.3 = (bf16[32,2560]{1,0:T(8,128)(2,1)S(1)}, bf16[32,2560]{1,0:T(8,128)(2,1)S(1)}, u32[]{:S(2)}, u32[]{:S(2)}) collective-permute-start(bf16[32,2560]{1,0:T(8,128)(2,1)S(1)} %maximum_maximum_fusion.1), channel_id=1, source_target_pairs={{0,60},{1,61},{2,62},{3,63},{4,0},{5,1},{6,2},{7,3},{8,4},{9,5},{1... | collective-permute-start | bytes 491528 | tf_op jit(solution)/shard_map/ppermute | solution.py:350
  31.1 5.1 collective-permute-start.4
  39.9 5.1 collective-permute-start.5
  48.3 5.1 collective-permute-start.7
  57.4 5.1 collective-permute-start.9
  66.0 2.7 collective-permute-start.10
  71.3 5.6 collective-permute-start.12
  77.6 4.3 collective-permute-start.24
  83.9 5.1 collective-permute-start.21
  90.9 3.0 collective-permute-done.10.refs_2_
  94.0 5.6 collective-permute-start.14
  99.6 11.8 %all-to-all-start = ((bf16[64,4,2048]{2,1,0:T(4,128)(2,1)}), bf16[64,4,2048]{2,1,0:T(4,128)(2,1)S(1)}, u32[]{:S(2)}, u32[]{:S(2)}) async-start(bf16[64,4,2048]{2,1,0:T(4,128)(2,1)} %reshape.239), calls=%async_computation | async-start | bytes 2097152 | tf_op jit(solution)/shard_map/all_to_all | solution.py:419
  114.6 3.4 collective-permute-start.15
  118.5 5.7 collective-permute-start.16
  125.5 23.2 %collective-permute-done.15 = bf16[16,2560]{1,0:T(8,128)(2,1)S(1)} collective-permute-done((bf16[16,2560]{1,0:T(8,128)(2,1)S(1)}, bf16[16,2560]{1,0:T(8,128)(2,1)S(1)}, u32[]{:S(2)}, u32[]{:S(2)}) %collective-permute-start.15) | collective-permute-done | bytes 81952 | tf_op jit(solution)/shard_map/ppermute | solution.py:353
  149.4 3.0 collective-permute-start.17
  152.3 2.9 collective-permute-start.18
  157.1 4.2 collective-permute-start.26
  168.3 5.1 collective-permute-start.22
  181.1 5.1 collective-permute-start.19
  191.3 3.1 collective-permute-done.27.refs_4_
  194.4 101.6 %shard_map.125 = (bf16[16,4,32,1536]{3,2,1,0:T(8,128)(2,1)}, bf16[16,4,16,2048]{3,2,1,0:T(8,128)(2,1)}) custom-call(s32[2]{0:T(128)} %pad_add_fusion.place_ref, bf16[5,32,2560]{2,1,0:T(8,128)(2,1)} %bitcast_dynamic-update-slice_fusion.refs_0_, bf16[5,32,2560]{2,1,0:T(8,128)(2,1)} %collective-permute-done.24.refs_1_, ...), custom_call_target="tpu_custom_call" | custom-call | tf_op jit(solution)/shard_map/pallas_call | solution.py:296
  296.0 121.6 %shard_map.126 = (bf16[16,4,32,1536]{3,2,1,0:T(8,128)(2,1)}, bf16[16,4,16,2048]{3,2,1,0:T(8,128)(2,1)}) custom-call(s32[2]{0:T(128)} %pad_add_fusion.place_ref, bf16[6,32,2560]{2,1,0:T(8,128)(2,1)} %bitcast_dynamic-update-slice_fusion.9.refs_0_, bf16[6,32,2560]{2,1,0:T(8,128)(2,1)} %collective-permute-done.21.refs_1_, ...), custom_call_target="tpu_custom_call", output_to_operand_aliasing={{0}: (6, {}), {1}: (7, {})} | custom-call | tf_op jit(solution)/shard_map/pallas_call | solution.py:296
  417.7 101.8 %shard_map.127 = (bf16[16,4,32,1536]{3,2,1,0:T(8,128)(2,1)}, bf16[16,4,16,2048]{3,2,1,0:T(8,128)(2,1)}) custom-call(s32[2]{0:T(128)} %pad_add_fusion.place_ref, bf16[5,32,2560]{2,1,0:T(8,128)(2,1)} %fusion.1.refs_0_, bf16[5,32,2560]{2,1,0:T(8,128)(2,1)} %collective-permute-done.17.refs_1_, ...), custom_call_target="tpu_custom_call", output_to_operand_aliasing={{0}: (6, {}), {1}: (7, {})} | custom-call | tf_op jit(solution)/shard_map/pallas_call | solution.py:296
  520.6 2.4 convolution_convert_fusion.1
  522.9 10.6 %conditional.16 = ((bf16[128,2048]{1,0:T(8,128)(2,1)}, bf16[128,2048]{1,0:T(8,128)(2,1)S(1)}, bf16[128,1024]{1,0:T(8,128)(2,1)}, bf16[128,256]{1,0:T(8,128)(2,1)...) conditional(s32[]{:T(128)} %convert_element_type.117, ...), branch_computations={%region_3.4_spmd, %region_4.5_spmd} | conditional | bytes 1998934 | solution.py:521
  525.2 8.4 branch_1_fun.16
  533.6 2.1 collective-permute-start.28
  542.8 3.5 collective-permute-start.33
  547.1 6.3 conditional.24
  556.4 4.9 conditional.26
  564.2 5.1 conditional.28
  572.3 4.5 conditional.30
  578.2 219.4 %collective-permute-done.41 = bf16[128,2048]{1,0:T(8,128)(2,1)S(1)} collective-permute-done((bf16[128,2048]{1,0:T(8,128)(2,1)}, bf16[128,2048]{1,0:T(8,128)(2,1)S(1)}, u32[]{:S(2)}, u32[]{:S(2)}) %collective-permute-start.41) | collective-permute-done | bytes 524320 | tf_op jit(solution)/shard_map/ppermute | solution.py:548
  797.6 10.4 %conditional.31 = ((bf16[128,1024]{1,0:T(8,128)(2,1)}, bf16[128,256]{1,0:T(8,128)(2,1)}, bf16[128,128]{1,0:T(8,128)(2,1)})) conditional(s32[]{:T(128)} %convert_element_type.117, (bf16[128,1024]{1,0:T(8,128)(2,1)}, bf16[128,256]{1,0:T(8,128)(2,1)}, bf16[128,128]{1,0:T(8,128)(2,1)}) %tuple.138, (bf16[128,2048]{1,0:T(8,128)(2,1)S(1)}, ...), branch_computations={%region_33.34_spmd, %region_34.35_spmd} | conditional | bytes 262176 | solution.py:546
  799.5 8.5 branch_1_fun.31
  811.6 4.5 collective-permute-done.42
  818.1 5.6 collective-permute-done.43
  825.6 4.1 collective-permute-done.44
  831.6 5.4 collective-permute-done.45
  837.1 4.2 collective-permute-start.46
  841.3 7.0 collective-permute-done.46
  848.4 7.8 collective-permute-start.47
  856.1 6.9 collective-permute-done.47
  865.0 5.5 collective-permute-done.48
  870.6 2.2 collective-permute-start.49
  872.8 4.3 collective-permute-done.49
  (174 shorter events, 104.0 us)
Async XLA Ops:
  4.3 24.2 %collective-permute-start = (bf16[32,2560]{1,0:T(8,128)(2,1)S(1)}, bf16[32,2560]{1,0:T(8,128)(2,1)S(1)}, u32[]{:S(2)}, u32[]{:S(2)}) collective-permute-start(bf16[32,2560]{1,0:T(8,128)(2,1)S(1)} %maximum_maximum_fusion.1), channel_id=1, source_target_pairs={{0,4},{1,5},{2,6},{3,7},{4,8},{5,9},{6,10},{7,11},{8,12},{9,13},{1... | collective-permute-start | bytes 491528 | tf_op jit(solution)/shard_map/ppermute | solution.py:349
  8.1 23.0 %collective-permute-start.3 = (bf16[32,2560]{1,0:T(8,128)(2,1)S(1)}, bf16[32,2560]{1,0:T(8,128)(2,1)S(1)}, u32[]{:S(2)}, u32[]{:S(2)}) collective-permute-start(bf16[32,2560]{1,0:T(8,128)(2,1)S(1)} %maximum_maximum_fusion.1), channel_id=1, source_target_pairs={{0,60},{1,61},{2,62},{3,63},{4,0},{5,1},{6,2},{7,3},{8,4},{9,5},{1... | collective-permute-start | bytes 491528 | tf_op jit(solution)/shard_map/ppermute | solution.py:350
  28.5 8.8 collective-permute-start.1
  31.1 8.8 collective-permute-start.4
  37.3 8.4 collective-permute-start.2
  39.9 8.4 collective-permute-start.5
  46.4 8.4 collective-permute-start.6
  48.3 9.1 %collective-permute-start.7 = (bf16[32,2560]{1,0:T(8,128)(2,1)S(1)}, bf16[32,2560]{1,0:T(8,128)(2,1)S(1)}, u32[]{:S(2)}, u32[]{:S(2)}) collective-permute-start(bf16[32,2560]{1,0:T(8,128)(2,1)S(1)} %collective-permute-done.5), channel_id=1, source_target_pairs={{0,60},{1,61},{2,62},{3,63},{4,0},{5,1},{6,2},{7,3},{8,4},{9,5},{1... | collective-permute-start | bytes 491528 | tf_op jit(solution)/shard_map/ppermute | solution.py:350
  54.8 8.4 collective-permute-start.8
  57.4 7.9 collective-permute-start.9
  66.0 28.0 %collective-permute-start.10 = (bf16[6,32,2560]{2,1,0:T(8,128)(2,1)}, bf16[6,32,2560]{2,1,0:T(8,128)(2,1)S(1)}, u32[]{:S(2)}, u32[]{:S(2)}) collective-permute-start(bf16[6,32,2560]{2,1,0:T(8,128)(2,1)} %bitcast_dynamic-update-slice_fusion.9.refs_0_), channel_id=1, source_target_pairs={{0,3},{1,0},{2,1},{3,2},{4,7},{5,4},{6,5},{7,6},{8,11},{9,8},{10,9... | collective-permute-start | bytes 2949128 | tf_op jit(solution)/shard_map/ppermute | solution.py:360
  69.4 14.4 %collective-permute-start.11 = (bf16[32,2560]{1,0:T(8,128)(2,1)S(1)}, bf16[32,2560]{1,0:T(8,128)(2,1)}, u32[]{:S(2)}, u32[]{:S(2)}) collective-permute-start(bf16[32,2560]{1,0:T(8,128)(2,1)S(1)} %collective-permute-done.8), channel_id=1, source_target_pairs={{0,4},{1,5},{2,6},{3,7},{4,8},{5,9},{6,10},{7,11},{8,12},{9,13},{1... | collective-permute-start | bytes 491528 | tf_op jit(solution)/shard_map/ppermute | solution.py:349
  71.3 17.7 %collective-permute-start.12 = (bf16[32,2560]{1,0:T(8,128)(2,1)S(1)}, bf16[32,2560]{1,0:T(8,128)(2,1)}, u32[]{:S(2)}, u32[]{:S(2)}) collective-permute-start(bf16[32,2560]{1,0:T(8,128)(2,1)S(1)} %collective-permute-done.9), channel_id=1, source_target_pairs={{0,60},{1,61},{2,62},{3,63},{4,0},{5,1},{6,2},{7,3},{8,4},{9,5},{1... | collective-permute-start | bytes 491528 | tf_op jit(solution)/shard_map/ppermute | solution.py:350
  77.6 78.5 %collective-permute-start.24 = (bf16[5,32,2560]{2,1,0:T(8,128)(2,1)}, bf16[5,32,2560]{2,1,0:T(8,128)(2,1)}, u32[]{:S(2)}, u32[]{:S(2)}) collective-permute-start(bf16[5,32,2560]{2,1,0:T(8,128)(2,1)} %bitcast_dynamic-update-slice_fusion.refs_0_), channel_id=1, source_target_pairs={{0,1},{1,2},{2,3},{3,0},{4,5},{5,6},{6,7},{7,4},{8,9},{9,10},{10,1... | collective-permute-start | bytes 2457608 | tf_op jit(solution)/shard_map/ppermute | solution.py:359
  81.9 86.4 %collective-permute-start.25 = (bf16[5,32,2560]{2,1,0:T(8,128)(2,1)}, bf16[5,32,2560]{2,1,0:T(8,128)(2,1)}, u32[]{:S(2)}, u32[]{:S(2)}) collective-permute-start(bf16[5,32,2560]{2,1,0:T(8,128)(2,1)} %bitcast_dynamic-update-slice_fusion.refs_0_), channel_id=1, source_target_pairs={{0,3},{1,0},{2,1},{3,2},{4,7},{5,4},{6,5},{7,6},{8,11},{9,8},{10,9... | collective-permute-start | bytes 2457608 | tf_op jit(solution)/shard_map/ppermute | solution.py:360
  83.9 80.7 %collective-permute-start.21 = (bf16[6,32,2560]{2,1,0:T(8,128)(2,1)}, bf16[6,32,2560]{2,1,0:T(8,128)(2,1)}, u32[]{:S(2)}, u32[]{:S(2)}) collective-permute-start(bf16[6,32,2560]{2,1,0:T(8,128)(2,1)} %bitcast_dynamic-update-slice_fusion.9.refs_0_), channel_id=1, source_target_pairs={{0,1},{1,2},{2,3},{3,0},{4,5},{5,6},{6,7},{7,4},{8,9},{9,10},{10,1... | collective-permute-start | bytes 2949128 | tf_op jit(solution)/shard_map/ppermute | solution.py:359
  89.0 25.5 %collective-permute-start.13 = (bf16[32,2560]{1,0:T(8,128)(2,1)}, bf16[32,2560]{1,0:T(8,128)(2,1)S(1)}, u32[]{:S(2)}, u32[]{:S(2)}) collective-permute-start(bf16[32,2560]{1,0:T(8,128)(2,1)} %collective-permute-done.11), channel_id=1, source_target_pairs={{0,4},{1,5},{2,6},{3,7},{4,8},{5,9},{6,10},{7,11},{8,12},{9,13},{1... | collective-permute-start | bytes 491528 | tf_op jit(solution)/shard_map/ppermute | solution.py:349
  94.0 24.5 %collective-permute-start.14 = (bf16[32,2560]{1,0:T(8,128)(2,1)}, bf16[32,2560]{1,0:T(8,128)(2,1)S(1)}, u32[]{:S(2)}, u32[]{:S(2)}) collective-permute-start(bf16[32,2560]{1,0:T(8,128)(2,1)} %collective-permute-done.12), channel_id=1, source_target_pairs={{0,60},{1,61},{2,62},{3,63},{4,0},{5,1},{6,2},{7,3},{8,4},{9,5},{1... | collective-permute-start | bytes 491528 | tf_op jit(solution)/shard_map/ppermute | solution.py:350
  99.6 419.8 %all-to-all-start = ((bf16[64,4,2048]{2,1,0:T(4,128)(2,1)}), bf16[64,4,2048]{2,1,0:T(4,128)(2,1)S(1)}, u32[]{:S(2)}, u32[]{:S(2)}) async-start(bf16[64,4,2048]{2,1,0:T(4,128)(2,1)} %reshape.239), calls=%async_computation | async-start | bytes 2097152 | tf_op jit(solution)/shard_map/all_to_all | solution.py:419
  114.6 34.1 %collective-permute-start.15 = (bf16[16,2560]{1,0:T(8,128)(2,1)S(1)}, bf16[16,2560]{1,0:T(8,128)(2,1)S(1)}, u32[]{:S(2)}, u32[]{:S(2)}) collective-permute-start(bf16[16,2560]{1,0:T(8,128)(2,1)S(1)} %slice.70), channel_id=1, source_target_pairs={{0,4},{1,5},{2,6},{3,7},{4,8},{5,9},{6,10},{7,11},{8,12},{9,13},{1... | collective-permute-start | bytes 245768 | tf_op jit(solution)/shard_map/ppermute | solution.py:353
  118.5 30.2 %collective-permute-start.16 = (bf16[16,2560]{1,0:T(8,128)(2,1)S(1)}, bf16[16,2560]{1,0:T(8,128)(2,1)S(1)}, u32[]{:S(2)}, u32[]{:S(2)}) collective-permute-start(bf16[16,2560]{1,0:T(8,128)(2,1)S(1)} %slice.71), channel_id=1, source_target_pairs={{0,60},{1,61},{2,62},{3,63},{4,0},{5,1},{6,2},{7,3},{8,4},{9,5},{1... | collective-permute-start | bytes 245768 | tf_op jit(solution)/shard_map/ppermute | solution.py:354
  149.4 28.0 %collective-permute-start.17 = (bf16[5,32,2560]{2,1,0:T(8,128)(2,1)}, bf16[5,32,2560]{2,1,0:T(8,128)(2,1)}, u32[]{:S(2)}, u32[]{:S(2)}) collective-permute-start(bf16[5,32,2560]{2,1,0:T(8,128)(2,1)} %fusion.1.refs_0_), channel_id=1, source_target_pairs={{0,1},{1,2},{2,3},{3,0},{4,5},{5,6},{6,7},{7,4},{8,9},{9,10},{10,1... | collective-permute-start | bytes 2457608 | tf_op jit(solution)/shard_map/ppermute | solution.py:359
  152.3 28.7 %collective-permute-start.18 = (bf16[5,32,2560]{2,1,0:T(8,128)(2,1)}, bf16[5,32,2560]{2,1,0:T(8,128)(2,1)}, u32[]{:S(2)}, u32[]{:S(2)}) collective-permute-start(bf16[5,32,2560]{2,1,0:T(8,128)(2,1)} %fusion.1.refs_0_), channel_id=1, source_target_pairs={{0,3},{1,0},{2,1},{3,2},{4,7},{5,4},{6,5},{7,6},{8,11},{9,8},{10,9... | collective-permute-start | bytes 2457608 | tf_op jit(solution)/shard_map/ppermute | solution.py:360
  157.1 30.9 %collective-permute-start.26 = (bf16[5,16,2560]{2,1,0:T(8,128)(2,1)S(1)}, bf16[5,16,2560]{2,1,0:T(8,128)(2,1)}, u32[]{:S(2)}, u32[]{:S(2)}) collective-permute-start(bf16[5,16,2560]{2,1,0:T(8,128)(2,1)S(1)} %slice.76), channel_id=1, source_target_pairs={{0,1},{1,2},{2,3},{3,0},{4,5},{5,6},{6,7},{7,4},{8,9},{9,10},{10,1... | collective-permute-start | bytes 1228808 | tf_op jit(solution)/shard_map/ppermute | solution.py:361
  164.5 131.5 %collective-permute-start.23 = (bf16[6,16,2560]{2,1,0:T(8,128)(2,1)}, bf16[6,16,2560]{2,1,0:T(8,128)(2,1)}, u32[]{:S(2)}, u32[]{:S(2)}) collective-permute-start(bf16[6,16,2560]{2,1,0:T(8,128)(2,1)} %slice.75), channel_id=1, source_target_pairs={{0,3},{1,0},{2,1},{3,2},{4,7},{5,4},{6,5},{7,6},{8,11},{9,8},{10,9... | collective-permute-start | bytes 1474568 | tf_op jit(solution)/shard_map/ppermute | solution.py:362
  168.3 127.7 %collective-permute-start.22 = (bf16[6,16,2560]{2,1,0:T(8,128)(2,1)}, bf16[6,16,2560]{2,1,0:T(8,128)(2,1)}, u32[]{:S(2)}, u32[]{:S(2)}) collective-permute-start(bf16[6,16,2560]{2,1,0:T(8,128)(2,1)} %slice.74), channel_id=1, source_target_pairs={{0,1},{1,2},{2,3},{3,0},{4,5},{5,6},{6,7},{7,4},{8,9},{9,10},{10,1... | collective-permute-start | bytes 1474568 | tf_op jit(solution)/shard_map/ppermute | solution.py:361
  177.4 17.0 %collective-permute-start.27 = (bf16[5,16,2560]{2,1,0:T(8,128)(2,1)S(1)}, bf16[5,16,2560]{2,1,0:T(8,128)(2,1)}, u32[]{:S(2)}, u32[]{:S(2)}) collective-permute-start(bf16[5,16,2560]{2,1,0:T(8,128)(2,1)S(1)} %slice.77), channel_id=1, source_target_pairs={{0,3},{1,0},{2,1},{3,2},{4,7},{5,4},{6,5},{7,6},{8,11},{9,8},{10,9... | collective-permute-start | bytes 1228808 | tf_op jit(solution)/shard_map/ppermute | solution.py:362
  181.1 236.6 %collective-permute-start.19 = (bf16[5,16,2560]{2,1,0:T(8,128)(2,1)}, bf16[5,16,2560]{2,1,0:T(8,128)(2,1)}, u32[]{:S(2)}, u32[]{:S(2)}) collective-permute-start(bf16[5,16,2560]{2,1,0:T(8,128)(2,1)} %slice.72), channel_id=1, source_target_pairs={{0,1},{1,2},{2,3},{3,0},{4,5},{5,6},{6,7},{7,4},{8,9},{9,10},{10,1... | collective-permute-start | bytes 1228808 | tf_op jit(solution)/shard_map/ppermute | solution.py:361
  188.0 229.6 %collective-permute-start.20 = (bf16[5,16,2560]{2,1,0:T(8,128)(2,1)}, bf16[5,16,2560]{2,1,0:T(8,128)(2,1)}, u32[]{:S(2)}, u32[]{:S(2)}) collective-permute-start(bf16[5,16,2560]{2,1,0:T(8,128)(2,1)} %slice.73), channel_id=1, source_target_pairs={{0,3},{1,0},{2,1},{3,2},{4,7},{5,4},{6,5},{7,6},{8,11},{9,8},{10,9... | collective-permute-start | bytes 1228808 | tf_op jit(solution)/shard_map/ppermute | solution.py:362
  533.6 3.2 collective-permute-start.28
  536.7 1.5 collective-permute-start.29
  538.2 1.7 collective-permute-start.30
  539.9 1.5 collective-permute-start.31
  542.8 3.5 collective-permute-start.33
  554.9 1.5 collective-permute-start.36
  561.3 1.5 collective-permute-start.37
  562.8 1.5 collective-permute-start.38
  569.4 1.5 collective-permute-start.39
  570.8 1.5 collective-permute-start.40
  576.8 220.7 %collective-permute-start.41 = (bf16[128,2048]{1,0:T(8,128)(2,1)}, bf16[128,2048]{1,0:T(8,128)(2,1)S(1)}, u32[]{:S(2)}, u32[]{:S(2)}) collective-permute-start(bf16[128,2048]{1,0:T(8,128)(2,1)} %get-tuple-element.952), channel_id=1, source_target_pairs={{64,0},{65,1},{66,2},{67,3},{68,4},{69,5},{70,6},{71,7},{72,8},{73... | collective-permute-start | bytes 1572872 | tf_op jit(solution)/shard_map/ppermute | solution.py:548
  809.6 6.5 collective-permute-start.42
  816.2 7.5 collective-permute-start.43
  823.7 6.0 collective-permute-start.44
  829.7 7.4 collective-permute-start.45
  837.1 11.3 %collective-permute-start.46 = (bf16[48,512]{1,0:T(8,128)(2,1)S(1)}, bf16[48,512]{1,0:T(8,128)(2,1)S(1)}, u32[]{:S(2)}, u32[]{:S(2)}) collective-permute-start(bf16[48,512]{1,0:T(8,128)(2,1)S(1)} %add_convert_fusion.2), channel_id=1, source_target_pairs={{0,16},{1,17},{2,18},{3,19},{4,20},{5,21},{6,22},{7,23},{8,24},{9,... | collective-permute-start | bytes 147464 | tf_op jit(solution)/shard_map/ppermute | solution.py:381
  848.4 14.7 %collective-permute-start.47 = (bf16[48,512]{1,0:T(8,128)(2,1)S(1)}, bf16[48,512]{1,0:T(8,128)(2,1)S(1)}, u32[]{:S(2)}, u32[]{:S(2)}) collective-permute-start(bf16[48,512]{1,0:T(8,128)(2,1)S(1)} %add_convert_fusion.1), channel_id=1, source_target_pairs={{0,32},{1,33},{2,34},{3,35},{4,36},{5,37},{6,38},{7,39},{8,40},{9,... | collective-permute-start | bytes 147464 | tf_op jit(solution)/shard_map/ppermute | solution.py:381
  863.1 7.5 collective-permute-start.48
  870.6 6.5 collective-permute-start.49
  (7 other events, 632.8 us)
